TPU v7x, 512 devices: a whole 4x4x16 slice. The times are simulated.
512 devices in a mesh: ctx: 128 (over z, y, core), ch: 4 (over x).
Axes of the slice: x: 4, y: 4, z: 16, core: 2. Of those that a mesh axis runs over, the one named last changes fastest.
Arguments:
- query_proj: bfloat16 [16384, 4096], P('ctx', 'ch'), may hold values from -6 to 6
- key_proj: bfloat16 [16384, 4096], P('ctx', 'ch'), may hold values from -6 to 6
- value_proj: bfloat16 [16384, 4096], P('ctx', 'ch'), may hold values from -6 to 6
- decay_scale: float32 [16, 4096], P(None, 'ch'), may hold values from 0.25 to 512
- residues: float32 [16, 4096], P(None, 'ch'), may hold values from -1.5 to 1.5
- skip_gain: float32 [4096], P('ch'), may hold values from -4 to 4
- out_weight: bfloat16 [4096, 4096], P('ctx', 'ch'), may hold values from -0.09375 to 0.09375
Outputs:
- mixed: bfloat16 [16384, 4096], P('ctx', 'ch')
All inputs are finite; a program needn't handle non-finite values.
Results may differ from a plain program's by a relative error of at most 0.019.
Values may be sent and summed in bfloat16 or wider, within the bound.
No kernel may reach another device: no remote copies, remote signals or barrier semaphores. Data moves between devices by JAX's collectives and lax.ppermute only.
A program may use at most 128 MiB of HBM per device.

v0:
```python
import jax
import jax.numpy as jnp
from jax import lax
from jax.sharding import PartitionSpec as P

MODES = 16


def circle(rows, cols, modulus):
    angle = rows[:, None] * cols[None, :] % modulus
    angle = angle.astype(jnp.float32) * (2.0 * jnp.pi / modulus)
    return (jnp.cos(angle), jnp.sin(angle))


def matmul(left, right):
    return jnp.dot(left, right, precision=lax.Precision.HIGHEST, preferred_element_type=jnp.float32)


def along(table, stacked):
    return jnp.einsum(
        "qb,jbw->jqw",
        table,
        stacked,
        precision=lax.Precision.HIGHEST,
        preferred_element_type=jnp.float32,
    )


def spectral_conv(product, decay_scale, residues):
    tokens, width = product.shape
    parts = lax.axis_size("ctx")
    here = lax.axis_index("ctx")
    inner = tokens // parts
    span = 2 * parts
    seq_len = tokens * parts
    total = 2 * seq_len
    spread = lax.all_to_all(
        product.reshape(1, tokens, width), "ctx", split_axis=1, concat_axis=0, tiled=True
    )
    flat = spread.astype(jnp.float32).reshape(parts, inner * width)
    span_ids = jnp.arange(span, dtype=jnp.int32)
    cos_a, sin_a = circle(span_ids, jnp.arange(parts, dtype=jnp.int32), span)
    real_a = matmul(cos_a, flat).reshape(span, inner, width)
    imag_a = -matmul(sin_a, flat).reshape(span, inner, width)
    local_b = here * inner + jnp.arange(inner, dtype=jnp.int32)
    cos_t, sin_t = circle(span_ids, local_b, total)
    cos_t = cos_t[:, :, None]
    sin_t = sin_t[:, :, None]
    twist_r = real_a * cos_t + imag_a * sin_t
    twist_i = imag_a * cos_t - real_a * sin_t
    gathered = lax.all_to_all(
        jnp.stack([twist_r, twist_i]).astype(jnp.bfloat16),
        "ctx",
        split_axis=1,
        concat_axis=2,
        tiled=True,
    ).astype(jnp.float32)
    token_ids = jnp.arange(tokens, dtype=jnp.int32)
    cos_b, sin_b = circle(token_ids, token_ids, tokens)
    spec_r = along(cos_b, gathered[0]) + along(sin_b, gathered[1])
    spec_i = along(cos_b, gathered[1]) - along(sin_b, gathered[0])
    own_rows = 2 * here + jnp.arange(2, dtype=jnp.int32)
    freq = own_rows[:, None] + span * token_ids[None, :]
    angle = freq.astype(jnp.float32) * (2.0 * jnp.pi / total)
    sin_f = jnp.sin(angle)[:, :, None]
    half_f = jnp.sin(0.5 * angle)[:, :, None]
    parity = (1 - 2 * (freq % 2)).astype(jnp.float32)[:, :, None]

    def add_mode(mode, carry):
        filt_r, filt_i = carry
        scale = decay_scale[mode][None, None, :]
        rate = scale / seq_len
        decay = jnp.exp(-rate)
        numer = (
            residues[mode][None, None, :] * jnp.sqrt(2.0 * rate) * (1.0 - parity * jnp.exp(-scale))
        )
        den_r = -jnp.expm1(-rate) + decay * 2.0 * half_f * half_f
        den_i = decay * sin_f
        modulus = den_r * den_r + den_i * den_i
        return (filt_r + numer * den_r / modulus, filt_i - numer * den_i / modulus)

    empty = jnp.zeros((2, tokens, width), jnp.float32)
    filt_r, filt_i = lax.fori_loop(0, MODES, add_mode, (empty, empty))
    prod_r = spec_r * filt_r - spec_i * filt_i
    prod_i = spec_r * filt_i + spec_i * filt_r
    back_r = along(cos_b, prod_r) - along(sin_b, prod_i)
    back_i = along(cos_b, prod_i) + along(sin_b, prod_r)
    cos_u, sin_u = circle(own_rows, token_ids, total)
    cos_u = cos_u[:, :, None]
    sin_u = sin_u[:, :, None]
    turn_r = back_r * cos_u - back_i * sin_u
    turn_i = back_r * sin_u + back_i * cos_u
    blocks = lax.all_to_all(
        jnp.stack([turn_r, turn_i]).astype(jnp.bfloat16),
        "ctx",
        split_axis=2,
        concat_axis=1,
        tiled=True,
    ).astype(jnp.float32)
    cos_c, sin_c = circle(jnp.arange(parts, dtype=jnp.int32), span_ids, span)
    conv = matmul(cos_c, blocks[0].reshape(span, inner * width)) - matmul(
        sin_c, blocks[1].reshape(span, inner * width)
    )
    conv = (conv / total).reshape(parts, inner, width).astype(jnp.bfloat16)
    return lax.all_to_all(conv, "ctx", split_axis=0, concat_axis=1, tiled=True).reshape(
        tokens, width
    )


def body(query_proj, key_proj, value_proj, decay_scale, residues, skip_gain, out_weight):
    product = (key_proj.astype(jnp.float32) * value_proj.astype(jnp.float32)).astype(jnp.bfloat16)
    conv = spectral_conv(product, decay_scale, residues)
    gated = (
        query_proj.astype(jnp.float32)
        * (conv.astype(jnp.float32) + skip_gain[None, :] * product.astype(jnp.float32))
    ).astype(jnp.bfloat16)
    contract = (((1,), (1,)), ((), ()))
    terms = lax.dot_general(
        gated,
        lax.all_gather(out_weight, "ctx", axis=0, tiled=True),
        contract,
        preferred_element_type=jnp.float32,
    )
    return lax.psum_scatter(terms.astype(jnp.bfloat16), "ch", scatter_dimension=1, tiled=True)


def solution(mesh):
    placed = (
        P("ctx", "ch"),
        P("ctx", "ch"),
        P("ctx", "ch"),
        P(None, "ch"),
        P(None, "ch"),
        P("ch"),
        P("ctx", "ch"),
    )
    return jax.shard_map(
        body, mesh=mesh, in_specs=placed, out_specs=P("ctx", "ch"), check_vma=False
    )
```

profile of v0, /device:TPU:1, one launch (start us, length us, event | category | flops | bytes accessed | tf_op | source)
XLA Modules:
  0.0 278.9 jit_solution(8453443936727610416)
XLA Ops:
  6.5 1.1 fusion.58
  8.6 2.1 reduce
  10.7 0.9 reshape.454
  11.6 20.6 %all-to-all-start = ((bf16[128,2,512]{2,1,0:T(2,128)(2,1)}), bf16[128,2,512]{2,1,0:T(2,128)(2,1)S(1)}, u32[]{:S(2)}, u32[]{:S(2)}) async-start(bf16[128,2,512]{2,1,0:T(2,128)(2,1)} %reshape.454), calls=%async_computation | async-start | bytes 524288 | tf_op jit(solution)/shard_map/all_to_all | solution.py:37
  33.0 19.6 %all-to-all-done = bf16[128,2,512]{2,1,0:T(2,128)(2,1)S(1)} async-done(((bf16[128,2,512]{2,1,0:T(2,128)(2,1)}), bf16[128,2,512]{2,1,0:T(2,128)(2,1)S(1)}, u32[]{:S(2)}, u32[]{:S(2)}) %all-to-all-start) | async-done | bytes 262176 | tf_op jit(solution)/shard_map/all_to_all | solution.py:37
  52.9 1.1 convolution_negate_fusion
  54.0 1.2 fusion.26
  55.3 2.1 copy.39
  57.5 8.3 %all-to-all-start.1 = ((bf16[2,256,1,1024]{3,0,2,1:T(2,128)(2,1)}), bf16[2,256,1,1024]{3,0,2,1:T(2,128)(2,1)S(1)}, u32[]{:S(2)}, u32[]{:S(2)}) async-start(bf16[2,256,1,1024]{3,0,2,1:T(2,128)(2,1)} %copy.39), calls=%async_computation.1 | async-start | bytes 2097152 | tf_op jit(solution)/shard_map/all_to_all | solution.py:51
  66.0 30.8 %while.20 = (s32[]{:T(128)}, f32[2,128,1024]{2,1,0:T(8,128)S(1)}, f32[2,128,1024]{2,1,0:T(8,128)S(1)}, f32[16,1024]{1,0:T(8,128)}, f32[16,1024]{1,0:T(8,128)}, /...) while((s32[]{:T(128)}, f32[2,128,1024]{2,1,0:T(8,128)S(1)}, ...), condition=%wide.region_1.2_spmd.clone.clone.clone, body=%wide.region_0.1_spmd.clone.clone.clone.sunk | while | flops 4730627 | bytes 4254843 | solution.py:83
  66.0 0.8 sqrt_multiply_fusion.2
  67.0 0.9 fusion.168
  69.0 0.9 fusion.168
  70.9 0.9 fusion.168
  71.8 0.8 sqrt_multiply_fusion.2
  72.8 0.9 fusion.168
  74.7 0.9 fusion.168
  76.7 0.9 fusion.168
  77.6 0.8 sqrt_multiply_fusion.2
  78.6 0.9 fusion.168
  80.5 0.9 fusion.168
  82.4 0.9 fusion.168
  84.4 0.9 fusion.168
  86.3 0.9 fusion.168
  88.2 0.9 fusion.168
  90.1 0.9 fusion.168
  92.1 0.9 fusion.168
  94.0 0.9 fusion.168
  95.9 0.9 fusion.168
  96.8 1.3 copy.41
  98.1 1.3 copy.42
  99.5 21.8 %all-to-all-done.1 = bf16[2,256,1,1024]{3,0,2,1:T(2,128)(2,1)S(1)} async-done(((bf16[2,256,1,1024]{3,0,2,1:T(2,128)(2,1)}), bf16[2,256,1,1024]{3,0,2,1:T(2,128)(2,1)S(1)}, u32[]{:S(2)}, u32[]{:S(2)}) %all-to-all-start.1) | async-done | bytes 1048608 | tf_op jit(solution)/shard_map/all_to_all | solution.py:51
  121.3 1.0 copy.40
  122.4 0.8 fusion.32
  123.2 0.8 fusion.33
  124.1 0.8 fusion.22
  124.9 2.3 multiply_subtract_fusion
  127.2 1.2 fusion.68
  128.4 1.2 fusion.70
  129.7 1.2 convolution_add_fusion
  130.9 1.4 fusion.28
  132.5 1.0 copy.45
  133.5 74.6 %all_to_all.48 = bf16[2,2,128,1024]{3,1,0,2:T(2,128)(2,1)S(1)} all-to-all(bf16[2,2,128,1024]{3,1,0,2:T(2,128)(2,1)S(1)} %copy.45), channel_id=1, replica_groups=mesh['ctx'=128,'ch'=4] {'ctx'}, dimensions={2} | all-to-all | bytes 2097152 | tf_op jit(solution)/shard_map/all_to_all | solution.py:93
  209.2 0.9 fusion.52
  210.1 0.9 fusion.25
  212.0 29.5 %all_to_all.49 = bf16[128,2,512]{2,1,0:T(2,128)(2,1)S(1)} all-to-all(bf16[128,2,512]{2,1,0:T(2,128)(2,1)S(1)} %reshape.456), channel_id=1, replica_groups=mesh['ctx'=128,'ch'=4] {'ctx'}, dimensions={0} | all-to-all | bytes 524288 | tf_op jit(solution)/shard_map/all_to_all | solution.py:105
  241.7 7.3 %convolution_convert_fusion = bf16[128,4096]{1,0:T(8,128)(2,1)} fusion(bf16[4096,1024]{1,0:T(8,128)(2,1)} %all-gather.2.cloned.1.call-done, bf16[128,1024]{1,0:T(8,128)(2,1)S(1)} %copy-done.3, bf16[128,1,1024]{2,1,0:T(2,128)(2,1)S(1)} %reshape.457, f32[1024]{0:T(1024)S(1)} %copy-done.4, bf16[128,1024]{1,0:T(8,128)(2,1)S(1)} %copy-done.1, ...), kind=kOutput, calls=%fused_computation.34 | convolution fusion | flops 1075707904 | bytes 10489856 | tf_op jit(solution)/shard_map/dot_general | solution.py:118
  249.1 23.0 %reduce-scatter.2.cloned.1.call-done = bf16[128,1024]{1,0:T(8,128)(2,1)} async-done(((bf16[128,4096]{1,0:T(8,128)(2,1)}), bf16[128,1024]{1,0:T(8,128)(2,1)}) %reduce-scatter.2.cloned.1.call-update) | async-done | bytes 262160 | tf_op jit(solution)/shard_map/reduce_scatter | solution.py:124
  (93 shorter events, 18.7 us)
Async XLA Ops:
  11.6 41.0 %all-to-all-start = ((bf16[128,2,512]{2,1,0:T(2,128)(2,1)}), bf16[128,2,512]{2,1,0:T(2,128)(2,1)S(1)}, u32[]{:S(2)}, u32[]{:S(2)}) async-start(bf16[128,2,512]{2,1,0:T(2,128)(2,1)} %reshape.454), calls=%async_computation | async-start | bytes 524288 | tf_op jit(solution)/shard_map/all_to_all | solution.py:37
  32.2 209.5 %all-gather.2.cloned.1.call-start = ((), (), s32[]{:S(2)}) async-start(), calls=%async_computation.5 | async-start | bytes 8454144 | tf_op jit(solution)/shard_map/all_gather | solution.py:120
  57.5 63.9 %all-to-all-start.1 = ((bf16[2,256,1,1024]{3,0,2,1:T(2,128)(2,1)}), bf16[2,256,1,1024]{3,0,2,1:T(2,128)(2,1)S(1)}, u32[]{:S(2)}, u32[]{:S(2)}) async-start(bf16[2,256,1,1024]{3,0,2,1:T(2,128)(2,1)} %copy.39), calls=%async_computation.1 | async-start | bytes 2097152 | tf_op jit(solution)/shard_map/all_to_all | solution.py:51
  65.8 206.3 %reduce-scatter.2.cloned.1.call-start = ((), (), s32[]{:S(2)}) async-start(), calls=%async_computation.6 | async-start | bytes 1310720 | tf_op jit(solution)/shard_map/reduce_scatter | solution.py:124
  98.1 26.8 %copy-start = (f32[2,128,1024]{1,2,0:T(8,128)S(1)}, f32[2,128,1024]{1,2,0:T(8,128)}, u32[]{:S(2)}) copy-start(f32[2,128,1024]{1,2,0:T(8,128)} %copy.41) | copy-start | bytes 3145732
  132.3 109.4 %copy-start.1 = (bf16[128,1024]{1,0:T(8,128)(2,1)S(1)}, bf16[128,1024]{1,0:T(8,128)(2,1)}, u32[]{:S(2)}) copy-start(bf16[128,1024]{1,0:T(8,128)(2,1)} %param.11) | copy-start | bytes 786436
  132.4 109.4 %copy-start.2 = (bf16[128,1024]{1,0:T(8,128)(2,1)S(1)}, bf16[128,1024]{1,0:T(8,128)(2,1)}, u32[]{:S(2)}) copy-start(bf16[128,1024]{1,0:T(8,128)(2,1)} %param.10) | copy-start | bytes 786436
  132.4 109.3 %copy-start.3 = (bf16[128,1024]{1,0:T(8,128)(2,1)S(1)}, bf16[128,1024]{1,0:T(8,128)(2,1)}, u32[]{:S(2)}) copy-start(bf16[128,1024]{1,0:T(8,128)(2,1)} %param.9) | copy-start | bytes 786436
  132.4 109.3 %copy-start.4 = (f32[1024]{0:T(1024)S(1)}, f32[1024]{0:T(1024)}, u32[]{:S(2)}) copy-start(f32[1024]{0:T(1024)} %param.14) | copy-start | bytes 12292
Sparse Core Ops, SparseCore 0:
  36.2 187.3 all-gather.1
  249.2 22.7 reduce-scatter.1
where the time goes:
time: 281 us; the launch traced here: 279 us
  blocking collectives  104 us (37%)
  waiting for transfers between devices  65.1 us (23%)
  other arithmetic  34.6 us (12%)
  starting transfers between devices  29.1 us (10%)
  matrix products  21.3 us (8%)
  between operations  13.7 us (5%)
  local copies, waits for them, and re-layouts  10.4 us (4%)
    all_to_all x1, blocking collectives, spectral_conv(): lax.all_to_all(jnp.stack([turn_r, turn_i]).astype(jnp.bfloat16), 'ctx', s...  74.6 us
    all_to_all x1, blocking collectives, spectral_conv(): lax.all_to_all(conv, 'ctx', split_axis=0, concat_axis=1, tiled=True)  29.5 us
    reduce_scatter x1, waiting for transfers between devices, body(): lax.psum_scatter(terms.astype(jnp.bfloat16), 'ch', scatter_dimension=1, t...  23 us
    all_to_all x1, waiting for transfers between devices, spectral_conv(): lax.all_to_all(jnp.stack([twist_r, twist_i]).astype(jnp.bfloat16), 'ctx',...  21.8 us
    all_to_all x1, starting transfers between devices, spectral_conv(): lax.all_to_all(product.reshape(1, tokens, width), 'ctx', split_axis=1, co...  20.6 us
    all_to_all x1, waiting for transfers between devices, spectral_conv(): lax.all_to_all(product.reshape(1, tokens, width), 'ctx', split_axis=1, co...  19.6 us
    sub x16, other arithmetic, add_mode(): return (filt_r + numer * den_r / modulus, filt_i - numer * den_i / modulus)  13.9 us
    mul x16, other arithmetic, add_mode(): residues[mode][None, None, :] * jnp.sqrt(2.0 * rate)  13.1 us
  transfers between devices with their start and end apart: 4, of which 3 were waited for; matrix products, arithmetic and copies ran while one was open for 19% of the time, Pallas kernels for 0%

commit v1 on v0

v1 whole, which is shorter than its diff:
```python
import jax
import jax.numpy as jnp
from jax import lax
from jax.experimental import pallas as pl
from jax.experimental.pallas import tpu as pltpu
from jax.sharding import Mesh
from jax.sharding import PartitionSpec as P

SEQ = 16384
F32 = jnp.float32
BF16 = jnp.bfloat16
VMEM = pl.BlockSpec(memory_space=pltpu.VMEM)
SMEM = pl.BlockSpec(memory_space=pltpu.SMEM)
PARAMS = pltpu.CompilerParams(vmem_limit_bytes=48 * 1024 * 1024)


def gain_of(scale, residues):
    return residues * jnp.sqrt(scale * (2.0 / SEQ))


def states_kernel(key_ref, value_ref, scale_ref, res_ref, out_ref, prod_ref):
    tokens, width = key_ref.shape
    modes = scale_ref.shape[0]
    product = key_ref[...].astype(F32) * value_ref[...].astype(F32)
    prod_ref[...] = product.astype(BF16).astype(F32)
    scale = scale_ref[...]
    decay = jnp.exp(scale * (-1.0 / SEQ))

    def step(t, state):
        return state * decay + prod_ref[pl.ds(t, 1), :]

    state = lax.fori_loop(0, tokens, step, jnp.zeros((modes, width), F32), unroll=8)
    state = state * gain_of(scale, res_ref[...])
    parts, _, lanes = out_ref.shape
    for part in range(parts):
        out_ref[part] = state[:, part * lanes : (part + 1) * lanes].astype(BF16)


def plane_kernel(states_ref, scale_ref, out_ref):
    parts = states_ref.shape[0]
    decay = jnp.exp(scale_ref[...] * (-1.0 / 128))
    total = states_ref[0].astype(F32)
    for part in range(1, parts):
        total = total * decay + states_ref[part].astype(F32)
    total = total.astype(BF16)
    for copy in range(out_ref.shape[0]):
        out_ref[copy] = total


def carry_kernel(plane_ref, totals_ref, states_ref, scale_ref, out_ref):
    plane = plane_ref[0]
    scale = scale_ref[...]
    decay = jnp.exp(scale * (-1.0 / 16))
    carry = jnp.zeros(scale.shape, F32)
    for other in range(totals_ref.shape[0]):
        carry = jnp.where(other < plane, carry * decay + totals_ref[other].astype(F32), carry)
    decay = jnp.exp(scale * (-1.0 / 128))
    for part in range(states_ref.shape[0]):
        out_ref[part] = carry.astype(BF16)
        carry = carry * decay + states_ref[part].astype(F32)


def gated_kernel(
    query_ref, key_ref, value_ref, scale_ref, res_ref, skip_ref, carry_ref, out_ref, prod_ref, conv_ref
):
    tokens, width = key_ref.shape
    parts, _, lanes = carry_ref.shape
    product = key_ref[...].astype(F32) * value_ref[...].astype(F32)
    prod_ref[...] = product.astype(BF16).astype(F32)
    scale = scale_ref[...]
    decay = jnp.exp(scale * (-1.0 / SEQ))
    gain = gain_of(scale, res_ref[...])
    start = jnp.concatenate([carry_ref[part].astype(F32) for part in range(parts)], axis=1)

    def step(t, state):
        state = state * decay + gain * prod_ref[pl.ds(t, 1), :]
        conv_ref[pl.ds(t, 1), :] = jnp.sum(state, axis=0, keepdims=True)
        return state

    lax.fori_loop(0, tokens, step, start, unroll=8)
    out_ref[...] = (
        query_ref[...].astype(F32) * (conv_ref[...] + skip_ref[...] * prod_ref[...])
    ).astype(BF16)


def project_kernel(gated_ref, weight_ref, out_ref):
    blocks = gated_ref.shape[0]
    pieces, _, lanes = out_ref.shape
    quarters = pieces // blocks
    for quarter in range(quarters):
        rows = weight_ref[quarter * lanes : (quarter + 1) * lanes, :]
        for block in range(blocks):
            out_ref[block * quarters + quarter] = lax.dot_general(
                gated_ref[block], rows, (((1,), (1,)), ((), ())), preferred_element_type=F32
            ).astype(BF16)


def sum_kernel(pieces_ref, out_ref):
    quarters = 4
    for row in range(quarters):
        total = pieces_ref[row * 4].astype(F32)
        for owner in range(1, 4):
            total = total + pieces_ref[row * 4 + owner].astype(F32)
        total = total.astype(BF16)
        for plane in range(4):
            start = plane * 256 + row * 64
            out_ref[:, start : start + 64] = total[:, plane * 64 : plane * 64 + 64]


def call(kernel, shape, inputs, specs=None, scratch=(), dtype=BF16):
    return pl.pallas_call(
        kernel,
        out_shape=jax.ShapeDtypeStruct(shape, dtype),
        in_specs=specs or [VMEM] * len(inputs),
        out_specs=VMEM,
        scratch_shapes=list(scratch),
        compiler_params=PARAMS,
    )(*inputs)


def exchange(pieces, axes):
    return lax.all_to_all(pieces, axes, split_axis=0, concat_axis=0, tiled=True)


def body(query, key, value, scale, residues, skip, out_weight):
    tokens, width = query.shape
    modes = scale.shape[0]
    near = ("y", "core")
    lanes = width // 8
    weight = lax.all_gather(out_weight, ("z", "core"), axis=0, tiled=True)
    work = pltpu.VMEM((tokens, width), F32)
    states = call(states_kernel, (8, modes, lanes), (key, value, scale, residues), scratch=[work])
    states = exchange(states, near)
    own = lax.axis_index(near)
    own_scale = lax.dynamic_slice_in_dim(scale, own * lanes, lanes, 1)
    totals = call(plane_kernel, (16, modes, lanes), (states, own_scale))
    totals = exchange(totals, "z")
    plane = lax.axis_index("z").astype(jnp.int32).reshape(1)
    carry = call(
        carry_kernel,
        (8, modes, lanes),
        (plane, totals, states, own_scale),
        specs=[SMEM, VMEM, VMEM, VMEM],
    )
    carry = exchange(carry, near)
    gated = call(
        gated_kernel,
        (tokens, width),
        (query, key, value, scale, residues, skip.reshape(1, width), carry),
        scratch=[work, work],
    )
    gated = exchange(jnp.broadcast_to(gated[None], (4, tokens, width)), "y")
    terms = call(project_kernel, (16, tokens, 256), (gated, weight))
    terms = exchange(terms, ("y", "x"))
    return call(sum_kernel, (tokens, width), (terms,))


def solution(mesh):
    fine = Mesh(mesh.devices.reshape(16, 4, 2, 4), ("z", "y", "core", "x"))
    both = P(("z", "y", "core"), "x")
    placed = (both, both, both, P(None, "x"), P(None, "x"), P("x"), both)
    return jax.shard_map(body, mesh=fine, in_specs=placed, out_specs=both, check_vma=False)
```

time: 281 us -> 123 us (0.44)
  blocking collectives: 104 us -> 48.2 us
  waiting for transfers between devices: 65.1 us -> 20.3 us
  other arithmetic: 34.6 us -> 0 us
  matrix products: 21.3 us -> 0 us
  Pallas kernels: 0 us -> 8.51 us
  starting transfers between devices: 29.1 us -> 20.9 us
    all_to_all x2 -> x3, blocking collectives: 104 us -> 48.2 us  [exchange(): return lax.all_to_all(pieces, axes, split_axis=0, concat_axis=0, tiled=True)]
    all_to_all x2, waiting for transfers between devices: 41.4 us -> 16.3 us  [exchange(): return lax.all_to_all(pieces, axes, split_axis=0, concat_axis=0, tiled=True)]
    reduce_scatter x1 -> x0, waiting for transfers between devices: 23 us -> none  [body(): lax.psum_scatter(terms.astype(jnp.bfloat16), 'ch', scatter_dimension=1, t...]
    dot_general x13 -> x0, matrix products: 21.3 us -> none  [the longest x8 9.9 us: along(): jnp.einsum('qb,jbw->jqw', table, stacked, precision=lax.Precision.HIGHEST...]
    mul x65 -> x0, other arithmetic: 16.3 us -> none  [the longest x16 13.1 us: add_mode(): residues[mode][None, None, :] * jnp.sqrt(2.0 * rate)]
    sub x16 -> x0, other arithmetic: 13.9 us -> none  [add_mode(): return (filt_r + numer * den_r / modulus, filt_i - numer * den_i / modulus)]
    pallas_call x0 -> x6, Pallas kernels: none -> 8.51 us  [call(): pl.pallas_call(kernel, out_shape=jax.ShapeDtypeStruct(shape, dtype), in_s...]
    unnamed x15 -> x22, local copies, waits for them, and re-layouts: 2.06 us -> 10.4 us
  transfers between devices with their start and end apart: 4 -> 3, of which waited for: 3 -> 3; matrix products, arithmetic and copies ran while one was open for 19% -> 1% of each run, Pallas kernels for 0% -> 4%
where the time goes in v1:
time: 123 us
  blocking collectives  48.2 us (39%)
  starting transfers between devices  20.9 us (17%)
  waiting for transfers between devices  20.3 us (17%)
  between operations  13.4 us (11%)
  local copies, waits for them, and re-layouts  11.2 us (9%)
  Pallas kernels  8.51 us (7%)
    all_to_all x3, blocking collectives, exchange(): return lax.all_to_all(pieces, axes, split_axis=0, concat_axis=0, tiled=True)  48.2 us
    all_to_all x2, starting transfers between devices, exchange(): return lax.all_to_all(pieces, axes, split_axis=0, concat_axis=0, tiled=True)  20.9 us
    all_to_all x2, waiting for transfers between devices, exchange(): return lax.all_to_all(pieces, axes, split_axis=0, concat_axis=0, tiled=True)  16.3 us
    unnamed x22, local copies, waits for them, and re-layouts  10.4 us
    pallas_call x6, Pallas kernels, call(): pl.pallas_call(kernel, out_shape=jax.ShapeDtypeStruct(shape, dtype), in_s...  8.51 us
    all_gather x1, waiting for transfers between devices, body(): weight = lax.all_gather(out_weight, ('z', 'core'), axis=0, tiled=True)  3.27 us
  transfers between devices with their start and end apart: 3, of which 3 were waited for; matrix products, arithmetic and copies ran while one was open for 1% of the time, Pallas kernels for 4%

profile of v1, /device:TPU:1, one launch (start us, length us, event | category | flops | bytes accessed | tf_op | source)
XLA Modules:
  0.0 122.6 jit_solution(9679698891195643407)
XLA Ops:
  6.5 0.0 all-gather.2.cloned.1.call-start
  6.5 0.7 all-gather.2.cloned.1.call-update
  7.3 0.0 copy-start.1
  7.3 0.9 copy-done.1
  8.2 0.0 copy-start.3
  8.2 0.9 copy-done.3
  9.2 0.0 copy-start.5
  9.2 0.8 copy-done.5
  10.0 0.0 copy-start.8
  10.0 0.8 copy-done.8
  10.8 1.5 %shard_map.73 = bf16[8,16,128]{2,1,0:T(8,128)(2,1)} custom-call(bf16[128,1024]{1,0:T(8,128)(2,1)S(1)} %copy-done.1, bf16[128,1024]{1,0:T(8,128)(2,1)S(1)} %copy-done.3, f32[16,1024]{1,0:T(8,128)S(1)} %copy-done.5, f32[16,1024]{1,0:T(8,128)S(1)} %copy-done.8), custom_call_target="tpu_custom_call" | custom-call | tf_op jit(solution)/shard_map/pallas_call | solution.py:111
  12.4 10.1 %all-to-all-start = ((bf16[8,16,128]{2,1,0:T(8,128)(2,1)}), bf16[8,16,128]{2,1,0:T(8,128)(2,1)S(1)}, u32[]{:S(2)}, u32[]{:S(2)}) async-start(bf16[8,16,128]{2,1,0:T(8,128)(2,1)} %shard_map.73), calls=%async_computation | async-start | bytes 65536 | tf_op jit(solution)/shard_map/all_to_all | solution.py:122
  22.5 0.7 constant_dynamic-slice_fusion.scale_ref
  23.2 4.0 %all-to-all-done.states_ref = bf16[8,16,128]{2,1,0:T(8,128)(2,1)S(1)} async-done(((bf16[8,16,128]{2,1,0:T(8,128)(2,1)}), bf16[8,16,128]{2,1,0:T(8,128)(2,1)S(1)}, u32[]{:S(2)}, u32[]{:S(2)}) %all-to-all-start) | async-done | bytes 32800 | tf_op jit(solution)/shard_map/all_to_all | solution.py:122
  27.2 0.7 shard_map.74
  27.9 10.7 %all-to-all-start.1 = ((bf16[16,16,128]{2,1,0:T(8,128)(2,1)}), bf16[16,16,128]{2,1,0:T(8,128)(2,1)S(1)}, u32[]{:S(2)}, u32[]{:S(2)}) async-start(bf16[16,16,128]{2,1,0:T(8,128)(2,1)} %shard_map.74), calls=%async_computation.1 | async-start | bytes 131072 | tf_op jit(solution)/shard_map/all_to_all | solution.py:122
  38.7 12.3 %all-to-all-done.1.totals_ref = bf16[16,16,128]{2,1,0:T(8,128)(2,1)S(1)} async-done(((bf16[16,16,128]{2,1,0:T(8,128)(2,1)}), bf16[16,16,128]{2,1,0:T(8,128)(2,1)S(1)}, u32[]{:S(2)}, u32[]{:S(2)}) %all-to-all-start.1) | async-done | bytes 65568 | tf_op jit(solution)/shard_map/all_to_all | solution.py:122
  51.0 0.1 shard_map.75
  51.0 9.1 %all_to_all.25.carry_ref = bf16[8,16,128]{2,1,0:T(8,128)(2,1)S(1)} all-to-all(bf16[8,16,128]{2,1,0:T(8,128)(2,1)S(1)} %shard_map.75), channel_id=1, replica_groups=mesh['z'=16,'y'=4,'core'=2,'x'=4] {'y','core'}, dimensions={0} | all-to-all | bytes 65536 | tf_op jit(solution)/shard_map/all_to_all | solution.py:122
  60.1 0.0 copy-start.2
  60.1 0.9 copy-done.2
  61.1 0.0 copy-start.4
  61.1 1.0 copy-done.4
  62.0 0.0 copy-start.6
  62.0 0.8 copy-done.6
  62.9 0.0 copy-start.7
  62.9 0.9 copy-done.7
  63.8 0.0 copy-start.9
  63.8 0.8 copy-done.9
  64.7 0.0 copy-start.10
  64.7 0.7 copy-done.10
  65.4 2.5 %shard_map.76 = bf16[128,1024]{1,0:T(8,128)(2,1)S(1)} custom-call(bf16[128,1024]{1,0:T(8,128)(2,1)S(1)} %copy-done.7, bf16[128,1024]{1,0:T(8,128)(2,1)S(1)} %copy-done.2, bf16[128,1024]{1,0:T(8,128)(2,1)S(1)} %copy-done.4, f32[16,1024]{1,0:T(8,128)S(1)} %copy-done.6, f32[16,1024]{1,0:T(8,128)S(1)} %copy-done.9, f32[1,1024]{1,0:T(1,128)S(1)} %bitcast.2, ...), custom_call_target="tpu_custom_call" | custom-call | tf_op jit(solution)/shard_map/pallas_call | solution.py:111
  67.9 0.1 broadcast_in_dim.2
  68.0 16.6 %all_to_all.26.gated_ref = bf16[4,128,1024]{2,1,0:T(8,128)(2,1)S(1)} all-to-all(bf16[4,128,1024]{2,1,0:T(8,128)(2,1)S(1)} %broadcast_in_dim.2), channel_id=1, replica_groups=mesh['z'=16,'y'=4,'core'=2,'x'=4] {'y'}, dimensions={0} | all-to-all | bytes 2097152 | tf_op jit(solution)/shard_map/all_to_all | solution.py:122
  84.6 3.3 %all-gather.2.cloned.1.call-done.weight_ref = bf16[1024,1024]{1,0:T(8,128)(2,1)} async-done(((bf16[32,1024]{1,0:T(8,128)(2,1)}), bf16[1024,1024]{1,0:T(8,128)(2,1)}) %all-gather.2.cloned.1.call-update) | async-done | bytes 2097168 | tf_op jit(solution)/shard_map/all_gather | solution.py:130
  87.9 0.0 copy-start
  87.9 1.6 %copy-done = bf16[1024,1024]{1,0:T(8,128)(2,1)S(1)} copy-done((bf16[1024,1024]{1,0:T(8,128)(2,1)S(1)}, bf16[1024,1024]{1,0:T(8,128)(2,1)}, u32[]{:S(2)}) %copy-start) | copy-done | bytes 2097176
  89.5 2.8 %shard_map.77 = bf16[16,128,256]{2,1,0:T(8,128)(2,1)S(1)} custom-call(bf16[4,128,1024]{2,1,0:T(8,128)(2,1)S(1)} %all_to_all.26.gated_ref, bf16[1024,1024]{1,0:T(8,128)(2,1)S(1)} %copy-done), custom_call_target="tpu_custom_call" | custom-call | tf_op jit(solution)/shard_map/pallas_call | solution.py:111
  92.3 22.6 %all_to_all.27.pieces_ref = bf16[16,128,256]{2,1,0:T(8,128)(2,1)S(1)} all-to-all(bf16[16,128,256]{2,1,0:T(8,128)(2,1)S(1)} %shard_map.77), channel_id=1, replica_groups=mesh['z'=16,'y'=4,'core'=2,'x'=4] {'y','x'}, dimensions={0} | all-to-all | bytes 2097152 | tf_op jit(solution)/shard_map/all_to_all | solution.py:122
  114.8 0.9 shard_map.78
Async XLA Ops:
  6.5 81.3 %all-gather.2.cloned.1.call-start = ((), (), s32[]{:S(2)}) async-start(), calls=%async_computation.5 | async-start | bytes 2162688 | tf_op jit(solution)/shard_map/all_gather | solution.py:130
  7.3 1.0 copy-start.1
  8.2 0.9 copy-start.3
  9.2 0.8 copy-start.5
  10.0 0.8 copy-start.8
  12.4 14.9 %all-to-all-start = ((bf16[8,16,128]{2,1,0:T(8,128)(2,1)}), bf16[8,16,128]{2,1,0:T(8,128)(2,1)S(1)}, u32[]{:S(2)}, u32[]{:S(2)}) async-start(bf16[8,16,128]{2,1,0:T(8,128)(2,1)} %shard_map.73), calls=%async_computation | async-start | bytes 65536 | tf_op jit(solution)/shard_map/all_to_all | solution.py:122
  27.9 23.1 %all-to-all-start.1 = ((bf16[16,16,128]{2,1,0:T(8,128)(2,1)}), bf16[16,16,128]{2,1,0:T(8,128)(2,1)S(1)}, u32[]{:S(2)}, u32[]{:S(2)}) async-start(bf16[16,16,128]{2,1,0:T(8,128)(2,1)} %shard_map.74), calls=%async_computation.1 | async-start | bytes 131072 | tf_op jit(solution)/shard_map/all_to_all | solution.py:122
  60.1 1.0 copy-start.2
  61.1 1.0 copy-start.4
  62.0 0.8 copy-start.6
  62.9 0.9 copy-start.7
  63.8 0.8 copy-start.9
  64.7 0.7 copy-start.10
  87.9 1.6 %copy-start = (bf16[1024,1024]{1,0:T(8,128)(2,1)S(1)}, bf16[1024,1024]{1,0:T(8,128)(2,1)}, u32[]{:S(2)}) copy-start(bf16[1024,1024]{1,0:T(8,128)(2,1)} %all-gather.2.cloned.1.call-done.weight_ref) | copy-start | bytes 6291460
Sparse Core Ops, SparseCore 0:
  9.5 78.3 all-gather.1

commit v2 on v1

v2 whole, which is shorter than its diff:
```python
import jax
import jax.numpy as jnp
from jax import lax
from jax.experimental import pallas as pl
from jax.experimental.pallas import tpu as pltpu
from jax.sharding import Mesh
from jax.sharding import PartitionSpec as P

SEQ = 16384
F32 = jnp.float32
BF16 = jnp.bfloat16
VMEM = pl.BlockSpec(memory_space=pltpu.VMEM)
HBM = pl.BlockSpec(memory_space=pltpu.HBM)
SMEM = pl.BlockSpec(memory_space=pltpu.SMEM)
NEAR = ("y", "core")
PLANES = ("zp", "zq")


def gain_of(scale, residues):
    return residues * jnp.sqrt(scale * (2.0 / SEQ))


def product_kernel(
    key_hbm, value_hbm, query_hbm, weight_hbm, out_ref, copy_hbm, key_ref, value_ref, query_ref, sems
):
    loads = [
        pltpu.make_async_copy(src, dst, sems.at[i])
        for i, (src, dst) in enumerate(
            ((key_hbm, key_ref), (value_hbm, value_ref), (query_hbm, query_ref), (weight_hbm, copy_hbm))
        )
    ]
    for load in loads:
        load.start()
    for load in loads[:3]:
        load.wait()
    tokens = key_ref.shape[0]
    parts, _, lanes = out_ref.shape
    for part in range(parts):
        cols = slice(part * lanes, (part + 1) * lanes)
        product = key_ref[:, cols].astype(F32) * value_ref[:, cols].astype(F32)
        out_ref[part, :tokens] = product.astype(BF16)
        out_ref[part, tokens:] = query_ref[:, cols]
    loads[3].wait()


def states_kernel(slices_ref, scale_ref, res_ref, totals_ref, states_ref, prod_ref):
    parts, tokens, lanes = prod_ref.shape
    modes = scale_ref.shape[0]
    prod_ref[...] = slices_ref[:, :tokens].astype(F32)
    scale = scale_ref[...]
    decay = jnp.exp(scale * (-1.0 / SEQ))
    gain = gain_of(scale, res_ref[...])

    def step(t, states):
        return tuple(
            state * decay + prod_ref[part, pl.ds(t, 1), :] for part, state in enumerate(states)
        )

    zero = jnp.zeros((modes, lanes), F32)
    states = lax.fori_loop(0, tokens, step, (zero,) * parts, unroll=8)
    decay = jnp.exp(scale * (-1.0 / 128))
    total = zero
    for part in range(parts):
        state = states[part] * gain
        states_ref[part] = state
        total = total * decay + state
    total = total.astype(BF16)
    for copy in range(totals_ref.shape[0]):
        totals_ref[copy] = total


def local_kernel(
    slices_ref, states_ref, scale_ref, res_ref, skip_ref, base_ref, powers_ref, prod_ref
):
    parts, tokens, lanes = prod_ref.shape
    modes = scale_ref.shape[0]
    prod_ref[...] = slices_ref[:, :tokens].astype(F32)
    scale = scale_ref[...]
    decay = jnp.exp(scale * (-1.0 / SEQ))
    gain = gain_of(scale, res_ref[...])
    leap = jnp.exp(scale * (-1.0 / 128))
    starts = [jnp.zeros((modes, lanes), F32)]
    for part in range(parts - 1):
        starts.append(starts[-1] * leap + states_ref[part])

    def step(t, states):
        fresh = []
        for part, state in enumerate(states):
            state = state * decay + gain * prod_ref[part, pl.ds(t, 1), :]
            base_ref[part, pl.ds(t, 1), :] = jnp.sum(state, axis=0, keepdims=True)
            fresh.append(state)
        return tuple(fresh)

    lax.fori_loop(0, tokens, step, tuple(starts), unroll=4)
    skip = skip_ref[...]
    for part in range(parts):
        base_ref[part] = base_ref[part] + skip * prod_ref[part]
    ages = (lax.broadcasted_iota(jnp.int32, (tokens, lanes), 0) + 1).astype(F32) * (-1.0 / SEQ)
    for mode in range(modes):
        powers_ref[mode] = jnp.exp(ages * scale[mode : mode + 1, :])


def gated_kernel(plane_ref, totals_ref, slices_ref, base_ref, powers_ref, scale_ref, out_ref):
    plane = plane_ref[0]
    parts, tokens, lanes = base_ref.shape
    modes = scale_ref.shape[0]
    scale = scale_ref[...]
    leap = jnp.exp(scale * (-1.0 / 16))
    carry = jnp.zeros(scale.shape, F32)
    for other in range(totals_ref.shape[0]):
        carry = jnp.where(other < plane, carry * leap + totals_ref[other].astype(F32), carry)
    leap = jnp.exp(scale * (-1.0 / 128))
    for part in range(parts):
        conv = base_ref[part]
        for mode in range(modes):
            conv = conv + powers_ref[mode] * carry[mode : mode + 1, :]
        gated = (slices_ref[part, tokens:].astype(F32) * conv).astype(BF16)
        for row in range(4):
            out_ref[2 * row + part % 2, part // 2] = gated
        carry = carry * leap


def project_kernel(gated_ref, weight_hbm, out_ref, rows_ref, weight_ref, sems):
    parts, blocks, tokens, lanes = gated_ref.shape
    loads = [
        pltpu.make_async_copy(
            weight_hbm.at[256 * quarter : 256 * quarter + 256], weight_ref.at[quarter], sems.at[quarter]
        )
        for quarter in range(4)
    ]
    for load in loads:
        load.start()
    for block in range(blocks):
        for part in range(parts):
            rows_ref[block * tokens : (block + 1) * tokens, part * lanes : (part + 1) * lanes] = (
                gated_ref[part, block]
            )
    order = [4 * far + 2 * core + near for far in range(2) for near in range(2) for core in range(2)]
    for quarter in range(4):
        loads[quarter].wait()
        weight = jnp.concatenate([weight_ref[quarter, 32 * i : 32 * i + 32, :] for i in order], axis=0)
        terms = lax.dot_general(
            rows_ref[...], weight, (((1,), (1,)), ((), ())), preferred_element_type=F32
        ).astype(BF16)
        for block in range(blocks):
            out_ref[block * 4 + quarter] = terms[block * tokens : (block + 1) * tokens]


def sum_kernel(pieces_ref, out_ref):
    for row in range(4):
        total = pieces_ref[row * 4].astype(F32)
        for owner in range(1, 4):
            total = total + pieces_ref[row * 4 + owner].astype(F32)
        total = total.astype(BF16)
        for plane in range(4):
            start = plane * 256 + row * 64
            out_ref[:, start : start + 64] = total[:, plane * 64 : plane * 64 + 64]


def call(kernel, outs, inputs, specs=None, scratch=(), cost=None, out_spec=None, limit=48):
    single = not isinstance(outs, list)
    return pl.pallas_call(
        kernel,
        out_shape=outs,
        in_specs=specs or [VMEM] * len(inputs),
        out_specs=out_spec or (VMEM if single else [VMEM] * len(outs)),
        scratch_shapes=list(scratch),
        compiler_params=pltpu.CompilerParams(vmem_limit_bytes=int(limit * 1024 * 1024)),
        cost_estimate=cost,
    )(*inputs)


def arr(*shape, dtype=BF16):
    return jax.ShapeDtypeStruct(shape, dtype)


def exchange(pieces, axes):
    return lax.all_to_all(pieces, axes, split_axis=0, concat_axis=0, tiled=True)


def body(query, key, value, scale, residues, skip, out_weight):
    tokens, width = query.shape
    modes = scale.shape[0]
    lanes = width // 8
    other = lax.ppermute(out_weight, "zq", [(0, 1), (1, 0)])
    z = lax.axis_index(PLANES).astype(jnp.int32)
    load = pltpu.VMEM((tokens, width), BF16)
    slices, same = call(
        product_kernel,
        [arr(8, 2 * tokens, lanes), arr(32, width)],
        (key, value, query, out_weight),
        specs=[HBM] * 4,
        scratch=[load, load, load, pltpu.SemaphoreType.DMA((4,))],
        out_spec=[VMEM, HBM],
        limit=62,
        cost=pl.CostEstimate(flops=2_000_000, bytes_accessed=4_000_000, transcendentals=0),
    )
    pair = jnp.where(
        z % 2 == 0, jnp.concatenate([same, other], axis=0), jnp.concatenate([other, same], axis=0)
    )
    weight = lax.all_gather(pair, ("zp", "core"), axis=0, tiled=True)
    slices = exchange(slices, NEAR)
    own = lax.axis_index(NEAR) * lanes
    scale, residues, skip = (
        lax.dynamic_slice_in_dim(a, own, lanes, 1) for a in (scale, residues, skip.reshape(1, width))
    )
    work = pltpu.VMEM((8, tokens, lanes), F32)
    totals, states = call(
        states_kernel,
        [arr(16, modes, lanes), arr(8, modes, lanes, dtype=F32)],
        (slices, scale, residues),
        scratch=[work],
    )
    totals = exchange(totals, PLANES)
    base, powers = call(
        local_kernel,
        [arr(8, tokens, lanes, dtype=F32), arr(modes, tokens, lanes, dtype=F32)],
        (slices, states, scale, residues, skip),
        scratch=[work],
        cost=pl.CostEstimate(flops=20_000_000, bytes_accessed=2_000_000, transcendentals=300_000),
    )
    gated = call(
        gated_kernel,
        arr(8, 4, tokens, lanes),
        (z.reshape(1), totals, slices, base, powers, scale),
        specs=[SMEM] + [VMEM] * 5,
    )
    gated = exchange(gated, NEAR)
    terms = call(
        project_kernel,
        arr(16, tokens, 256),
        (gated, weight),
        specs=[VMEM, HBM],
        scratch=[
            pltpu.VMEM((4 * tokens, width), BF16),
            pltpu.VMEM((4, 256, width), BF16),
            pltpu.SemaphoreType.DMA((4,)),
        ],
        limit=50.5,
    )
    terms = exchange(terms, ("y", "x"))
    return call(sum_kernel, arr(tokens, width), (terms,))


def solution(mesh):
    fine = Mesh(mesh.devices.reshape(8, 2, 4, 2, 4), ("zp", "zq", "y", "core", "x"))
    both = P(("zp", "zq", "y", "core"), "x")
    placed = (both, both, both, P(None, "x"), P(None, "x"), P("x"), both)
    return jax.shard_map(body, mesh=fine, in_specs=placed, out_specs=both, check_vma=False)
```

time: 123 us -> 113 us (0.919)
  local copies, waits for them, and re-layouts: 11.2 us -> 0.8 us
  blocking collectives: 48.2 us -> 40 us
  Pallas kernels: 8.51 us -> 13 us
  starting transfers between devices: 20.9 us -> 23.9 us
  other arithmetic: 0 us -> 1.61 us
  waiting for transfers between devices: 20.3 us -> 18.9 us
    unnamed x22 -> x2, local copies, waits for them, and re-layouts: 10.4 us -> 0.01 us
    all_to_all x3 -> x2, blocking collectives: 48.2 us -> 40 us  [exchange(): return lax.all_to_all(pieces, axes, split_axis=0, concat_axis=0, tiled=True)]
    ppermute x0 -> x1, starting transfers between devices: none -> 4.49 us  [body(): other = lax.ppermute(out_weight, 'zq', [(0, 1), (1, 0)])]
    pallas_call x6, Pallas kernels: 8.51 us -> 13 us  [call(): pl.pallas_call(kernel, out_shape=outs, in_specs=specs or [VMEM] * len(inp...]
    all_gather x1, waiting for transfers between devices: 3.27 us -> 0.01 us  [body(): weight = lax.all_gather(pair, ('zp', 'core'), axis=0, tiled=True)]
    all_to_all x2, waiting for transfers between devices: 16.3 us -> 18.9 us  [exchange(): return lax.all_to_all(pieces, axes, split_axis=0, concat_axis=0, tiled=True)]
    select_n x0 -> x1, other arithmetic: none -> 1.61 us  [body(): jnp.where(z % 2 == 0, jnp.concatenate([same, other], axis=0), jnp.concate...]
    all_to_all x2, starting transfers between devices: 20.9 us -> 19.4 us  [exchange(): return lax.all_to_all(pieces, axes, split_axis=0, concat_axis=0, tiled=True)]
  transfers between devices with their start and end apart: 3 -> 4, of which waited for: 3 -> 2; matrix products, arithmetic and copies ran while one was open for 1% -> 1% of each run, Pallas kernels for 4% -> 7%
where the time goes in v2:
time: 113 us; the launch traced here: 112 us
  blocking collectives  40 us (35%)
  starting transfers between devices  23.9 us (21%)
  waiting for transfers between devices  18.9 us (17%)
  between operations  13.5 us (12%)
  Pallas kernels  13 us (12%)
  other arithmetic  1.61 us (1%)
    all_to_all x2, blocking collectives, exchange(): return lax.all_to_all(pieces, axes, split_axis=0, concat_axis=0, tiled=True)  40 us
    all_to_all x2, starting transfers between devices, exchange(): return lax.all_to_all(pieces, axes, split_axis=0, concat_axis=0, tiled=True)  19.4 us
    all_to_all x2, waiting for transfers between devices, exchange(): return lax.all_to_all(pieces, axes, split_axis=0, concat_axis=0, tiled=True)  18.9 us
    pallas_call x6, Pallas kernels, call(): pl.pallas_call(kernel, out_shape=outs, in_specs=specs or [VMEM] * len(inp...  13 us
    ppermute x1, starting transfers between devices, body(): other = lax.ppermute(out_weight, 'zq', [(0, 1), (1, 0)])  4.49 us
  transfers between devices with their start and end apart: 4, of which 2 were waited for; matrix products, arithmetic and copies ran while one was open for 1% of the time, Pallas kernels for 7%

profile of v2, /device:TPU:1, one launch (start us, length us, event | category | flops | bytes accessed | tf_op | source)
XLA Modules:
  0.0 111.7 jit_solution(14695571019744148540)
XLA Ops:
  6.5 0.0 copy-start
  6.5 0.0 all-gather.2.cloned.1.call-start
  6.5 4.5 %collective-permute-start = (bf16[32,1024]{1,0:T(8,128)(2,1)}, bf16[32,1024]{1,0:T(8,128)(2,1)S(1)}, u32[]{:S(2)}, u32[]{:S(2)}) collective-permute-start(bf16[32,1024]{1,0:T(8,128)(2,1)} %weight_hbm.1), channel_id=1, source_target_pairs={{0,32},{32,0},{1,33},{33,1},{2,34},{34,2},{3,35},{35,3},{4,36},{36... | collective-permute-start | bytes 196616 | tf_op jit(solution)/shard_map/ppermute | solution.py:185
  11.1 3.9 %shard_map.73 = (bf16[8,256,128]{2,1,0:T(8,128)(2,1)}, bf16[32,1024]{1,0:T(8,128)(2,1)}) custom-call(bf16[128,1024]{1,0:T(8,128)(2,1)} %key_hbm.1, bf16[128,1024]{1,0:T(8,128)(2,1)} %value_hbm.1, bf16[128,1024]{1,0:T(8,128)(2,1)} %query_hbm.1, bf16[32,1024]{1,0:T(8,128)(2,1)} %weight_hbm.1), custom_call_target="tpu_custom_call" | custom-call | flops 2000000 | bytes 4000000 | tf_op jit(solution)/shard_map/pallas_call | solution.py:162
  15.0 0.0 collective-permute-done
  15.0 1.6 %maximum_select_fusion = bf16[64,1024]{1,0:T(8,128)(2,1)} fusion(bf16[32,1024]{1,0:T(8,128)(2,1)S(1)} %collective-permute-done, bf16[32,1024]{1,0:T(8,128)(2,1)} %get-tuple-element.16, pred[]{:T(512)S(6)} %eq.5), kind=kLoop, calls=%fused_computation | loop fusion | flops 589824 | bytes 262145 | tf_op jit(solution)/shard_map/jit(_where)/select_n | solution.py:198
  16.6 0.0 all-gather.2.cloned.1.call-update
  16.6 8.3 %all-to-all-start = ((bf16[8,256,128]{2,1,0:T(8,128)(2,1)}), bf16[8,256,128]{2,1,0:T(8,128)(2,1)S(1)}, u32[]{:S(2)}, u32[]{:S(2)}) async-start(bf16[8,256,128]{2,1,0:T(8,128)(2,1)} %get-tuple-element.11), calls=%async_computation | async-start | bytes 1048576 | tf_op jit(solution)/shard_map/all_to_all | solution.py:178
  24.9 0.7 constant_dynamic-slice_fusion
  25.7 8.8 %all-to-all-done.slices_ref = bf16[8,256,128]{2,1,0:T(8,128)(2,1)S(1)} async-done(((bf16[8,256,128]{2,1,0:T(8,128)(2,1)}), bf16[8,256,128]{2,1,0:T(8,128)(2,1)S(1)}, u32[]{:S(2)}, u32[]{:S(2)}) %all-to-all-start) | async-done | bytes 524320 | tf_op jit(solution)/shard_map/all_to_all | solution.py:178
  34.4 1.3 %shard_map.74 = (bf16[16,16,128]{2,1,0:T(8,128)(2,1)}, f32[8,16,128]{2,1,0:T(8,128)S(1)}) custom-call(bf16[8,256,128]{2,1,0:T(8,128)(2,1)S(1)} %all-to-all-done.slices_ref, f32[16,128]{1,0:T(8,128)S(1)} %get-tuple-element.18.scale_ref, f32[16,128]{1,0:T(8,128)S(1)} %get-tuple-element.17.res_ref), custom_call_target="tpu_custom_call" | custom-call | tf_op jit(solution)/shard_map/pallas_call | solution.py:162
  35.7 11.1 %all-to-all-start.1 = ((bf16[16,16,128]{2,1,0:T(8,128)(2,1)}), bf16[16,16,128]{2,1,0:T(8,128)(2,1)S(1)}, u32[]{:S(2)}, u32[]{:S(2)}) async-start(bf16[16,16,128]{2,1,0:T(8,128)(2,1)} %get-tuple-element.12), calls=%async_computation.1 | async-start | bytes 131072 | tf_op jit(solution)/shard_map/all_to_all | solution.py:178
  46.9 0.0 copy-done
  46.9 0.1 dynamic-slice_bitcast_fusion.skip_ref
  47.0 2.2 %shard_map.75 = (f32[8,128,128]{2,1,0:T(8,128)S(1)}, f32[16,128,128]{2,1,0:T(8,128)S(1)}) custom-call(bf16[8,256,128]{2,1,0:T(8,128)(2,1)S(1)} %all-to-all-done.slices_ref, f32[8,16,128]{2,1,0:T(8,128)S(1)} %get-tuple-element.13.states_ref, f32[16,128]{1,0:T(8,128)S(1)} %get-tuple-element.18.scale_ref, f32[16,128]{1,0:T(8,128)S(1)} %get-tuple-element.17.res_ref, ...), custom_call_target="tpu_custom_call" | custom-call | flops 20000000 | bytes 2000000 | tf_op jit(solution)/shard_map/pallas_call | solution.py:162
  49.2 10.1 %all-to-all-done.1.totals_ref = bf16[16,16,128]{2,1,0:T(8,128)(2,1)S(1)} async-done(((bf16[16,16,128]{2,1,0:T(8,128)(2,1)}), bf16[16,16,128]{2,1,0:T(8,128)(2,1)S(1)}, u32[]{:S(2)}, u32[]{:S(2)}) %all-to-all-start.1) | async-done | bytes 65568 | tf_op jit(solution)/shard_map/all_to_all | solution.py:178
  59.3 0.7 shard_map.76
  60.0 20.1 %all_to_all.20.gated_ref = bf16[8,4,128,128]{3,2,1,0:T(8,128)(2,1)S(1)} all-to-all(bf16[8,4,128,128]{3,2,1,0:T(8,128)(2,1)S(1)} %shard_map.76), channel_id=1, replica_groups=mesh['zp'=8,'zq'=2,'y'=4,'core'=2,'x'=4] {'y','core'}, dimensions={0} | all-to-all | bytes 2097152 | tf_op jit(solution)/shard_map/all_to_all | solution.py:178
  80.1 0.0 all-gather.2.cloned.1.call-done.weight_hbm
  80.1 4.0 %shard_map.77 = bf16[16,128,256]{2,1,0:T(8,128)(2,1)S(1)} custom-call(bf16[8,4,128,128]{3,2,1,0:T(8,128)(2,1)S(1)} %all_to_all.20.gated_ref, bf16[1024,1024]{1,0:T(8,128)(2,1)} %all-gather.2.cloned.1.call-done.weight_hbm), custom_call_target="tpu_custom_call" | custom-call | tf_op jit(solution)/shard_map/pallas_call | solution.py:162
  84.1 19.8 %all_to_all.21.pieces_ref = bf16[16,128,256]{2,1,0:T(8,128)(2,1)S(1)} all-to-all(bf16[16,128,256]{2,1,0:T(8,128)(2,1)S(1)} %shard_map.77), channel_id=1, replica_groups=mesh['zp'=8,'zq'=2,'y'=4,'core'=2,'x'=4] {'y','x'}, dimensions={0} | all-to-all | bytes 2097152 | tf_op jit(solution)/shard_map/all_to_all | solution.py:178
  103.9 0.9 shard_map.78
Async XLA Ops:
  6.5 40.3 %copy-start = (f32[1024]{0:T(1024)S(1)}, f32[1024]{0:T(1024)}, u32[]{:S(2)}) copy-start(f32[1024]{0:T(1024)} %param.12) | copy-start | bytes 12292
  6.5 73.6 %all-gather.2.cloned.1.call-start = ((), (), s32[]{:S(2)}) async-start(), calls=%async_computation.4 | async-start | bytes 2228224 | tf_op jit(solution)/shard_map/all_gather | solution.py:201
  6.5 8.5 %collective-permute-start = (bf16[32,1024]{1,0:T(8,128)(2,1)}, bf16[32,1024]{1,0:T(8,128)(2,1)S(1)}, u32[]{:S(2)}, u32[]{:S(2)}) collective-permute-start(bf16[32,1024]{1,0:T(8,128)(2,1)} %weight_hbm.1), channel_id=1, source_target_pairs={{0,32},{32,0},{1,33},{33,1},{2,34},{34,2},{3,35},{35,3},{4,36},{36... | collective-permute-start | bytes 196616 | tf_op jit(solution)/shard_map/ppermute | solution.py:185
  16.6 17.8 %all-to-all-start = ((bf16[8,256,128]{2,1,0:T(8,128)(2,1)}), bf16[8,256,128]{2,1,0:T(8,128)(2,1)S(1)}, u32[]{:S(2)}, u32[]{:S(2)}) async-start(bf16[8,256,128]{2,1,0:T(8,128)(2,1)} %get-tuple-element.11), calls=%async_computation | async-start | bytes 1048576 | tf_op jit(solution)/shard_map/all_to_all | solution.py:178
  35.7 23.6 %all-to-all-start.1 = ((bf16[16,16,128]{2,1,0:T(8,128)(2,1)}), bf16[16,16,128]{2,1,0:T(8,128)(2,1)S(1)}, u32[]{:S(2)}, u32[]{:S(2)}) async-start(bf16[16,16,128]{2,1,0:T(8,128)(2,1)} %get-tuple-element.12), calls=%async_computation.1 | async-start | bytes 131072 | tf_op jit(solution)/shard_map/all_to_all | solution.py:178
Sparse Core Ops, SparseCore 0:
  16.8 59.2 all-gather.1

commit v3 on v2

--- a/solution.py
+++ b/solution.py
@@ -21,17 +21,17 @@
 
 
 def product_kernel(
-    key_hbm, value_hbm, query_hbm, weight_hbm, out_ref, copy_hbm, key_ref, value_ref, query_ref, sems
+    key_hbm, value_hbm, query_hbm, weight_hbm, out_ref, copy_ref, key_ref, value_ref, query_ref, weight_ref, sems
 ):
     loads = [
         pltpu.make_async_copy(src, dst, sems.at[i])
         for i, (src, dst) in enumerate(
-            ((key_hbm, key_ref), (value_hbm, value_ref), (query_hbm, query_ref), (weight_hbm, copy_hbm))
+            ((key_hbm, key_ref), (value_hbm, value_ref), (query_hbm, query_ref), (weight_hbm, weight_ref))
         )
     ]
     for load in loads:
         load.start()
-    for load in loads[:3]:
+    for load in loads:
         load.wait()
     tokens = key_ref.shape[0]
     parts, _, lanes = out_ref.shape
@@ -40,7 +40,7 @@
         product = key_ref[:, cols].astype(F32) * value_ref[:, cols].astype(F32)
         out_ref[part, :tokens] = product.astype(BF16)
         out_ref[part, tokens:] = query_ref[:, cols]
-    loads[3].wait()
+    copy_ref[...] = weight_ref[...]
 
 
 def states_kernel(slices_ref, scale_ref, res_ref, totals_ref, states_ref, prod_ref):
@@ -136,14 +136,21 @@
                 gated_ref[part, block]
             )
     order = [4 * far + 2 * core + near for far in range(2) for near in range(2) for core in range(2)]
-    for quarter in range(4):
-        loads[quarter].wait()
-        weight = jnp.concatenate([weight_ref[quarter, 32 * i : 32 * i + 32, :] for i in order], axis=0)
+    for half in range(2):
+        quarters = (2 * half, 2 * half + 1)
+        for quarter in quarters:
+            loads[quarter].wait()
+        weight = jnp.concatenate(
+            [weight_ref[quarter, 32 * i : 32 * i + 32, :] for quarter in quarters for i in order], axis=0
+        )
         terms = lax.dot_general(
             rows_ref[...], weight, (((1,), (1,)), ((), ())), preferred_element_type=F32
         ).astype(BF16)
-        for block in range(blocks):
-            out_ref[block * 4 + quarter] = terms[block * tokens : (block + 1) * tokens]
+        for i, quarter in enumerate(quarters):
+            for block in range(blocks):
+                out_ref[block * 4 + quarter] = terms[
+                    block * tokens : (block + 1) * tokens, 256 * i : 256 * i + 256
+                ]
 
 
 def sum_kernel(pieces_ref, out_ref):
@@ -182,7 +189,6 @@
     tokens, width = query.shape
     modes = scale.shape[0]
     lanes = width // 8
-    other = lax.ppermute(out_weight, "zq", [(0, 1), (1, 0)])
     z = lax.axis_index(PLANES).astype(jnp.int32)
     load = pltpu.VMEM((tokens, width), BF16)
     slices, same = call(
@@ -190,13 +196,15 @@
         [arr(8, 2 * tokens, lanes), arr(32, width)],
         (key, value, query, out_weight),
         specs=[HBM] * 4,
-        scratch=[load, load, load, pltpu.SemaphoreType.DMA((4,))],
-        out_spec=[VMEM, HBM],
+        scratch=[load, load, load, pltpu.VMEM((32, width), BF16), pltpu.SemaphoreType.DMA((4,))],
         limit=62,
         cost=pl.CostEstimate(flops=2_000_000, bytes_accessed=4_000_000, transcendentals=0),
     )
+    other = lax.ppermute(out_weight, "zq", [(0, 1), (1, 0)])
     pair = jnp.where(
-        z % 2 == 0, jnp.concatenate([same, other], axis=0), jnp.concatenate([other, same], axis=0)
+        z % 2 == 0,
+        jnp.concatenate([same, other], axis=0),
+        jnp.concatenate([other, same], axis=0),
     )
     weight = lax.all_gather(pair, ("zp", "core"), axis=0, tiled=True)
     slices = exchange(slices, NEAR)
@@ -210,6 +218,7 @@
         [arr(16, modes, lanes), arr(8, modes, lanes, dtype=F32)],
         (slices, scale, residues),
         scratch=[work],
+        cost=pl.CostEstimate(flops=20_000_000, bytes_accessed=2_000_000, transcendentals=0),
     )
     totals = exchange(totals, PLANES)
     base, powers = call(

time: 113 us -> 111 us (0.982)
  Pallas kernels: 13 us -> 9.89 us
  starting transfers between devices: 23.9 us -> 25.2 us
    pallas_call x6, Pallas kernels: 13 us -> 9.89 us  [call(): pl.pallas_call(kernel, out_shape=outs, in_specs=specs or [VMEM] * len(inp...]
    all_to_all x2, starting transfers between devices: 19.4 us -> 20.8 us  [exchange(): return lax.all_to_all(pieces, axes, split_axis=0, concat_axis=0, tiled=True)]
  transfers between devices with their start and end apart: 4 -> 4, of which waited for: 2 -> 2; matrix products, arithmetic and copies ran while one was open for 1% -> 1% of each run, Pallas kernels for 7% -> 6%
where the time goes in v3:
time: 111 us; the launch traced here: 110 us
  blocking collectives  40 us (36%)
  starting transfers between devices  25.2 us (23%)
  waiting for transfers between devices  18.9 us (17%)
  between operations  13.5 us (12%)
  Pallas kernels  9.89 us (9%)
  other arithmetic  1.61 us (1%)
    all_to_all x2, blocking collectives, exchange(): return lax.all_to_all(pieces, axes, split_axis=0, concat_axis=0, tiled=True)  40 us
    all_to_all x2, starting transfers between devices, exchange(): return lax.all_to_all(pieces, axes, split_axis=0, concat_axis=0, tiled=True)  20.8 us
    all_to_all x2, waiting for transfers between devices, exchange(): return lax.all_to_all(pieces, axes, split_axis=0, concat_axis=0, tiled=True)  18.9 us
    pallas_call x6, Pallas kernels, call(): pl.pallas_call(kernel, out_shape=outs, in_specs=specs or [VMEM] * len(inp...  9.89 us
    ppermute x1, starting transfers between devices, body(): other = lax.ppermute(out_weight, 'zq', [(0, 1), (1, 0)])  4.49 us
  transfers between devices with their start and end apart: 4, of which 2 were waited for; matrix products, arithmetic and copies ran while one was open for 1% of the time, Pallas kernels for 6%

profile of v3, /device:TPU:1, one launch (start us, length us, event | category | flops | bytes accessed | tf_op | source)
XLA Modules:
  0.0 110.0 jit_solution(2831710658584922773)
XLA Ops:
  6.5 0.0 copy-start
  6.5 0.0 all-gather.2.cloned.1.call-start
  6.5 4.5 %collective-permute-start = (bf16[32,1024]{1,0:T(8,128)(2,1)}, bf16[32,1024]{1,0:T(8,128)(2,1)S(1)}, u32[]{:S(2)}, u32[]{:S(2)}) collective-permute-start(bf16[32,1024]{1,0:T(8,128)(2,1)} %weight_hbm.1), channel_id=1, source_target_pairs={{0,32},{32,0},{1,33},{33,1},{2,34},{34,2},{3,35},{35,3},{4,36},{36... | collective-permute-start | bytes 196616 | tf_op jit(solution)/shard_map/ppermute | solution.py:203
  11.1 2.1 %shard_map.73 = (bf16[8,256,128]{2,1,0:T(8,128)(2,1)}, bf16[32,1024]{1,0:T(8,128)(2,1)}) custom-call(bf16[128,1024]{1,0:T(8,128)(2,1)} %key_hbm.1, bf16[128,1024]{1,0:T(8,128)(2,1)} %value_hbm.1, bf16[128,1024]{1,0:T(8,128)(2,1)} %query_hbm.1, bf16[32,1024]{1,0:T(8,128)(2,1)} %weight_hbm.1), custom_call_target="tpu_custom_call" | custom-call | flops 2000000 | bytes 4000000 | tf_op jit(solution)/shard_map/pallas_call | solution.py:169
  13.1 0.0 collective-permute-done
  13.2 1.6 %maximum_select_fusion = bf16[64,1024]{1,0:T(8,128)(2,1)} fusion(bf16[32,1024]{1,0:T(8,128)(2,1)S(1)} %collective-permute-done, bf16[32,1024]{1,0:T(8,128)(2,1)} %get-tuple-element.16, pred[]{:T(512)S(6)} %eq.5), kind=kLoop, calls=%fused_computation | loop fusion | flops 589824 | bytes 262145 | tf_op jit(solution)/shard_map/jit(_where)/select_n | solution.py:204
  14.8 0.0 all-gather.2.cloned.1.call-update
  14.8 10.2 %all-to-all-start = ((bf16[8,256,128]{2,1,0:T(8,128)(2,1)}), bf16[8,256,128]{2,1,0:T(8,128)(2,1)S(1)}, u32[]{:S(2)}, u32[]{:S(2)}) async-start(bf16[8,256,128]{2,1,0:T(8,128)(2,1)} %get-tuple-element.11), calls=%async_computation | async-start | bytes 1048576 | tf_op jit(solution)/shard_map/all_to_all | solution.py:185
  24.9 0.7 constant_dynamic-slice_fusion
  25.7 8.8 %all-to-all-done.slices_ref = bf16[8,256,128]{2,1,0:T(8,128)(2,1)S(1)} async-done(((bf16[8,256,128]{2,1,0:T(8,128)(2,1)}), bf16[8,256,128]{2,1,0:T(8,128)(2,1)S(1)}, u32[]{:S(2)}, u32[]{:S(2)}) %all-to-all-start) | async-done | bytes 524320 | tf_op jit(solution)/shard_map/all_to_all | solution.py:185
  34.4 1.3 %shard_map.74 = (bf16[16,16,128]{2,1,0:T(8,128)(2,1)}, f32[8,16,128]{2,1,0:T(8,128)S(1)}) custom-call(bf16[8,256,128]{2,1,0:T(8,128)(2,1)S(1)} %all-to-all-done.slices_ref, f32[16,128]{1,0:T(8,128)S(1)} %get-tuple-element.18.scale_ref, f32[16,128]{1,0:T(8,128)S(1)} %get-tuple-element.17.res_ref), custom_call_target="tpu_custom_call" | custom-call | flops 20000000 | bytes 2000000 | tf_op jit(solution)/shard_map/pallas_call | solution.py:169
  35.7 10.6 %all-to-all-start.1 = ((bf16[16,16,128]{2,1,0:T(8,128)(2,1)}), bf16[16,16,128]{2,1,0:T(8,128)(2,1)S(1)}, u32[]{:S(2)}, u32[]{:S(2)}) async-start(bf16[16,16,128]{2,1,0:T(8,128)(2,1)} %get-tuple-element.12), calls=%async_computation.1 | async-start | bytes 131072 | tf_op jit(solution)/shard_map/all_to_all | solution.py:185
  46.3 0.0 copy-done
  46.3 0.1 dynamic-slice_bitcast_fusion.skip_ref
  46.4 2.2 %shard_map.75 = (f32[8,128,128]{2,1,0:T(8,128)S(1)}, f32[16,128,128]{2,1,0:T(8,128)S(1)}) custom-call(bf16[8,256,128]{2,1,0:T(8,128)(2,1)S(1)} %all-to-all-done.slices_ref, f32[8,16,128]{2,1,0:T(8,128)S(1)} %get-tuple-element.13.states_ref, f32[16,128]{1,0:T(8,128)S(1)} %get-tuple-element.18.scale_ref, f32[16,128]{1,0:T(8,128)S(1)} %get-tuple-element.17.res_ref, ...), custom_call_target="tpu_custom_call" | custom-call | flops 20000000 | bytes 2000000 | tf_op jit(solution)/shard_map/pallas_call | solution.py:169
  48.6 10.1 %all-to-all-done.1.totals_ref = bf16[16,16,128]{2,1,0:T(8,128)(2,1)S(1)} async-done(((bf16[16,16,128]{2,1,0:T(8,128)(2,1)}), bf16[16,16,128]{2,1,0:T(8,128)(2,1)S(1)}, u32[]{:S(2)}, u32[]{:S(2)}) %all-to-all-start.1) | async-done | bytes 65568 | tf_op jit(solution)/shard_map/all_to_all | solution.py:185
  58.8 0.7 shard_map.76
  59.4 20.1 %all_to_all.20.gated_ref = bf16[8,4,128,128]{3,2,1,0:T(8,128)(2,1)S(1)} all-to-all(bf16[8,4,128,128]{3,2,1,0:T(8,128)(2,1)S(1)} %shard_map.76), channel_id=1, replica_groups=mesh['zp'=8,'zq'=2,'y'=4,'core'=2,'x'=4] {'y','core'}, dimensions={0} | all-to-all | bytes 2097152 | tf_op jit(solution)/shard_map/all_to_all | solution.py:185
  79.5 0.0 all-gather.2.cloned.1.call-done.weight_hbm
  79.6 2.7 %shard_map.77 = bf16[16,128,256]{2,1,0:T(8,128)(2,1)S(1)} custom-call(bf16[8,4,128,128]{3,2,1,0:T(8,128)(2,1)S(1)} %all_to_all.20.gated_ref, bf16[1024,1024]{1,0:T(8,128)(2,1)} %all-gather.2.cloned.1.call-done.weight_hbm), custom_call_target="tpu_custom_call" | custom-call | tf_op jit(solution)/shard_map/pallas_call | solution.py:169
  82.3 19.9 %all_to_all.21.pieces_ref = bf16[16,128,256]{2,1,0:T(8,128)(2,1)S(1)} all-to-all(bf16[16,128,256]{2,1,0:T(8,128)(2,1)S(1)} %shard_map.77), channel_id=1, replica_groups=mesh['zp'=8,'zq'=2,'y'=4,'core'=2,'x'=4] {'y','x'}, dimensions={0} | all-to-all | bytes 2097152 | tf_op jit(solution)/shard_map/all_to_all | solution.py:185
  102.2 0.9 shard_map.78
Async XLA Ops:
  6.5 39.8 %copy-start = (f32[1024]{0:T(1024)S(1)}, f32[1024]{0:T(1024)}, u32[]{:S(2)}) copy-start(f32[1024]{0:T(1024)} %param.12) | copy-start | bytes 12292
  6.5 73.0 %all-gather.2.cloned.1.call-start = ((), (), s32[]{:S(2)}) async-start(), calls=%async_computation.4 | async-start | bytes 2228224 | tf_op jit(solution)/shard_map/all_gather | solution.py:209
  6.5 6.6 %collective-permute-start = (bf16[32,1024]{1,0:T(8,128)(2,1)}, bf16[32,1024]{1,0:T(8,128)(2,1)S(1)}, u32[]{:S(2)}, u32[]{:S(2)}) collective-permute-start(bf16[32,1024]{1,0:T(8,128)(2,1)} %weight_hbm.1), channel_id=1, source_target_pairs={{0,32},{32,0},{1,33},{33,1},{2,34},{34,2},{3,35},{35,3},{4,36},{36... | collective-permute-start | bytes 196616 | tf_op jit(solution)/shard_map/ppermute | solution.py:203
  14.8 19.7 %all-to-all-start = ((bf16[8,256,128]{2,1,0:T(8,128)(2,1)}), bf16[8,256,128]{2,1,0:T(8,128)(2,1)S(1)}, u32[]{:S(2)}, u32[]{:S(2)}) async-start(bf16[8,256,128]{2,1,0:T(8,128)(2,1)} %get-tuple-element.11), calls=%async_computation | async-start | bytes 1048576 | tf_op jit(solution)/shard_map/all_to_all | solution.py:185
  35.7 23.0 %all-to-all-start.1 = ((bf16[16,16,128]{2,1,0:T(8,128)(2,1)}), bf16[16,16,128]{2,1,0:T(8,128)(2,1)S(1)}, u32[]{:S(2)}, u32[]{:S(2)}) async-start(bf16[16,16,128]{2,1,0:T(8,128)(2,1)} %get-tuple-element.12), calls=%async_computation.1 | async-start | bytes 131072 | tf_op jit(solution)/shard_map/all_to_all | solution.py:185
Sparse Core Ops, SparseCore 0:
  14.9 61.2 all-gather.1

commit v4 on v3

--- a/solution.py
+++ b/solution.py
@@ -21,7 +21,18 @@
 
 
 def product_kernel(
-    key_hbm, value_hbm, query_hbm, weight_hbm, out_ref, copy_ref, key_ref, value_ref, query_ref, weight_ref, sems
+    near_ref,
+    key_hbm,
+    value_hbm,
+    query_hbm,
+    weight_hbm,
+    out_ref,
+    pair_hbm,
+    key_ref,
+    value_ref,
+    query_ref,
+    weight_ref,
+    sems,
 ):
     loads = [
         pltpu.make_async_copy(src, dst, sems.at[i])
@@ -33,6 +44,10 @@
         load.start()
     for load in loads:
         load.wait()
+    rows = weight_hbm.shape[0]
+    half = pair_hbm.at[pl.ds(pl.multiple_of(near_ref[0] * rows, rows), rows)]
+    store = pltpu.make_async_copy(weight_ref, half, sems.at[4])
+    store.start()
     tokens = key_ref.shape[0]
     parts, _, lanes = out_ref.shape
     for part in range(parts):
@@ -40,7 +55,7 @@
         product = key_ref[:, cols].astype(F32) * value_ref[:, cols].astype(F32)
         out_ref[part, :tokens] = product.astype(BF16)
         out_ref[part, tokens:] = query_ref[:, cols]
-    copy_ref[...] = weight_ref[...]
+    store.wait()
 
 
 def states_kernel(slices_ref, scale_ref, res_ref, totals_ref, states_ref, prod_ref):
@@ -191,21 +206,18 @@
     lanes = width // 8
     z = lax.axis_index(PLANES).astype(jnp.int32)
     load = pltpu.VMEM((tokens, width), BF16)
-    slices, same = call(
+    near = z.reshape(1) % 2
+    slices, half = call(
         product_kernel,
-        [arr(8, 2 * tokens, lanes), arr(32, width)],
-        (key, value, query, out_weight),
-        specs=[HBM] * 4,
-        scratch=[load, load, load, pltpu.VMEM((32, width), BF16), pltpu.SemaphoreType.DMA((4,))],
+        [arr(8, 2 * tokens, lanes), arr(64, width)],
+        (near, key, value, query, out_weight),
+        specs=[SMEM] + [HBM] * 4,
+        scratch=[load, load, load, pltpu.VMEM((32, width), BF16), pltpu.SemaphoreType.DMA((5,))],
         limit=62,
         cost=pl.CostEstimate(flops=2_000_000, bytes_accessed=4_000_000, transcendentals=0),
     )
     other = lax.ppermute(out_weight, "zq", [(0, 1), (1, 0)])
-    pair = jnp.where(
-        z % 2 == 0,
-        jnp.concatenate([same, other], axis=0),
-        jnp.concatenate([other, same], axis=0),
-    )
+    pair = lax.dynamic_update_slice_in_dim(half, other, (1 - z % 2) * out_weight.shape[0], 0)
     weight = lax.all_gather(pair, ("zp", "core"), axis=0, tiled=True)
     slices = exchange(slices, NEAR)
     own = lax.axis_index(NEAR) * lanes

time: 111 us -> 110 us (level)
  other arithmetic: 1.61 us -> 0 us
    select_n x1 -> x0, other arithmetic: 1.61 us -> none  [body(): jnp.where(z % 2 == 0, jnp.concatenate([same, other], axis=0), jnp.concate...]
where the time goes in v4:
time: 110 us; the launch traced here: 109 us
  blocking collectives  40 us (36%)
  starting transfers between devices  25.2 us (23%)
  waiting for transfers between devices  18.9 us (17%)
  between operations  13.5 us (12%)
  Pallas kernels  9.96 us (9%)
  local copies, waits for them, and re-layouts  1.44 us (1%)
    all_to_all x2, blocking collectives, exchange(): return lax.all_to_all(pieces, axes, split_axis=0, concat_axis=0, tiled=True)  40 us
    all_to_all x2, starting transfers between devices, exchange(): return lax.all_to_all(pieces, axes, split_axis=0, concat_axis=0, tiled=True)  20.7 us
    all_to_all x2, waiting for transfers between devices, exchange(): return lax.all_to_all(pieces, axes, split_axis=0, concat_axis=0, tiled=True)  18.9 us
    pallas_call x6, Pallas kernels, call(): pl.pallas_call(kernel, out_shape=outs, in_specs=specs or [VMEM] * len(inp...  9.96 us
    ppermute x1, starting transfers between devices, body(): other = lax.ppermute(out_weight, 'zq', [(0, 1), (1, 0)])  4.49 us
  transfers between devices with their start and end apart: 4, of which 2 were waited for; matrix products, arithmetic and copies ran while one was open for 1% of the time, Pallas kernels for 6%

profile of v4, /device:TPU:1, one launch (start us, length us, event | category | flops | bytes accessed | tf_op | source)
XLA Modules:
  0.0 109.0 jit_solution(2524059624202248324)
XLA Ops:
  6.5 0.0 copy-start
  6.5 0.0 all-gather.2.cloned.1.call-start
  6.5 4.5 %collective-permute-start = (bf16[32,1024]{1,0:T(8,128)(2,1)}, bf16[32,1024]{1,0:T(8,128)(2,1)S(1)}, u32[]{:S(2)}, u32[]{:S(2)}) collective-permute-start(bf16[32,1024]{1,0:T(8,128)(2,1)} %weight_hbm.1), channel_id=1, source_target_pairs={{0,32},{32,0},{1,33},{33,1},{2,34},{34,2},{3,35},{35,3},{4,36},{36... | collective-permute-start | bytes 196616 | tf_op jit(solution)/shard_map/ppermute | solution.py:219
  11.1 2.1 %shard_map.73 = (bf16[8,256,128]{2,1,0:T(8,128)(2,1)}, bf16[64,1024]{1,0:T(8,128)(2,1)}) custom-call(s32[1]{0:T(128)S(6)} %select_n.21.near_ref, bf16[128,1024]{1,0:T(8,128)(2,1)} %key_hbm.1, bf16[128,1024]{1,0:T(8,128)(2,1)} %value_hbm.1, bf16[128,1024]{1,0:T(8,128)(2,1)} %query_hbm.1, bf16[32,1024]{1,0:T(8,128)(2,1)} %weight_hbm.1), custom_call_target="tpu_custom_call" | custom-call | flops 2000000 | bytes 4000000 | tf_op jit(solution)/shard_map/pallas_call | solution.py:184
  13.2 0.0 collective-permute-done
  13.2 0.6 constant_dynamic-update-slice_fusion
  13.9 0.0 all-gather.2.cloned.1.call-update
  13.9 10.1 %all-to-all-start = ((bf16[8,256,128]{2,1,0:T(8,128)(2,1)}), bf16[8,256,128]{2,1,0:T(8,128)(2,1)S(1)}, u32[]{:S(2)}, u32[]{:S(2)}) async-start(bf16[8,256,128]{2,1,0:T(8,128)(2,1)} %get-tuple-element.11), calls=%async_computation | async-start | bytes 1048576 | tf_op jit(solution)/shard_map/all_to_all | solution.py:200
  24.0 0.7 constant_dynamic-slice_fusion
  24.7 8.8 %all-to-all-done.slices_ref = bf16[8,256,128]{2,1,0:T(8,128)(2,1)S(1)} async-done(((bf16[8,256,128]{2,1,0:T(8,128)(2,1)}), bf16[8,256,128]{2,1,0:T(8,128)(2,1)S(1)}, u32[]{:S(2)}, u32[]{:S(2)}) %all-to-all-start) | async-done | bytes 524320 | tf_op jit(solution)/shard_map/all_to_all | solution.py:200
  33.5 1.3 %shard_map.74 = (bf16[16,16,128]{2,1,0:T(8,128)(2,1)}, f32[8,16,128]{2,1,0:T(8,128)S(1)}) custom-call(bf16[8,256,128]{2,1,0:T(8,128)(2,1)S(1)} %all-to-all-done.slices_ref, f32[16,128]{1,0:T(8,128)S(1)} %get-tuple-element.18.scale_ref, f32[16,128]{1,0:T(8,128)S(1)} %get-tuple-element.17.res_ref), custom_call_target="tpu_custom_call" | custom-call | flops 20000000 | bytes 2000000 | tf_op jit(solution)/shard_map/pallas_call | solution.py:184
  34.8 10.6 %all-to-all-start.1 = ((bf16[16,16,128]{2,1,0:T(8,128)(2,1)}), bf16[16,16,128]{2,1,0:T(8,128)(2,1)S(1)}, u32[]{:S(2)}, u32[]{:S(2)}) async-start(bf16[16,16,128]{2,1,0:T(8,128)(2,1)} %get-tuple-element.12), calls=%async_computation.1 | async-start | bytes 131072 | tf_op jit(solution)/shard_map/all_to_all | solution.py:200
  45.4 0.0 copy-done
  45.4 0.1 dynamic-slice_bitcast_fusion.skip_ref
  45.5 2.2 %shard_map.75 = (f32[8,128,128]{2,1,0:T(8,128)S(1)}, f32[16,128,128]{2,1,0:T(8,128)S(1)}) custom-call(bf16[8,256,128]{2,1,0:T(8,128)(2,1)S(1)} %all-to-all-done.slices_ref, f32[8,16,128]{2,1,0:T(8,128)S(1)} %get-tuple-element.13.states_ref, f32[16,128]{1,0:T(8,128)S(1)} %get-tuple-element.18.scale_ref, f32[16,128]{1,0:T(8,128)S(1)} %get-tuple-element.17.res_ref, ...), custom_call_target="tpu_custom_call" | custom-call | flops 20000000 | bytes 2000000 | tf_op jit(solution)/shard_map/pallas_call | solution.py:184
  47.7 10.1 %all-to-all-done.1.totals_ref = bf16[16,16,128]{2,1,0:T(8,128)(2,1)S(1)} async-done(((bf16[16,16,128]{2,1,0:T(8,128)(2,1)}), bf16[16,16,128]{2,1,0:T(8,128)(2,1)S(1)}, u32[]{:S(2)}, u32[]{:S(2)}) %all-to-all-start.1) | async-done | bytes 65568 | tf_op jit(solution)/shard_map/all_to_all | solution.py:200
  57.8 0.7 shard_map.76
  58.5 20.1 %all_to_all.20.gated_ref = bf16[8,4,128,128]{3,2,1,0:T(8,128)(2,1)S(1)} all-to-all(bf16[8,4,128,128]{3,2,1,0:T(8,128)(2,1)S(1)} %shard_map.76), channel_id=1, replica_groups=mesh['zp'=8,'zq'=2,'y'=4,'core'=2,'x'=4] {'y','core'}, dimensions={0} | all-to-all | bytes 2097152 | tf_op jit(solution)/shard_map/all_to_all | solution.py:200
  78.6 0.0 all-gather.2.cloned.1.call-done.weight_hbm
  78.6 2.7 %shard_map.77 = bf16[16,128,256]{2,1,0:T(8,128)(2,1)S(1)} custom-call(bf16[8,4,128,128]{3,2,1,0:T(8,128)(2,1)S(1)} %all_to_all.20.gated_ref, bf16[1024,1024]{1,0:T(8,128)(2,1)} %all-gather.2.cloned.1.call-done.weight_hbm), custom_call_target="tpu_custom_call" | custom-call | tf_op jit(solution)/shard_map/pallas_call | solution.py:184
  81.3 19.9 %all_to_all.21.pieces_ref = bf16[16,128,256]{2,1,0:T(8,128)(2,1)S(1)} all-to-all(bf16[16,128,256]{2,1,0:T(8,128)(2,1)S(1)} %shard_map.77), channel_id=1, replica_groups=mesh['zp'=8,'zq'=2,'y'=4,'core'=2,'x'=4] {'y','x'}, dimensions={0} | all-to-all | bytes 2097152 | tf_op jit(solution)/shard_map/all_to_all | solution.py:200
  101.2 0.9 shard_map.78
Async XLA Ops:
  6.5 38.8 %copy-start = (f32[1024]{0:T(1024)S(1)}, f32[1024]{0:T(1024)}, u32[]{:S(2)}) copy-start(f32[1024]{0:T(1024)} %param.12) | copy-start | bytes 12292
  6.5 72.0 %all-gather.2.cloned.1.call-start = ((), (), s32[]{:S(2)}) async-start(), calls=%async_computation.4 | async-start | bytes 2228224 | tf_op jit(solution)/shard_map/all_gather | solution.py:221
  6.5 6.7 %collective-permute-start = (bf16[32,1024]{1,0:T(8,128)(2,1)}, bf16[32,1024]{1,0:T(8,128)(2,1)S(1)}, u32[]{:S(2)}, u32[]{:S(2)}) collective-permute-start(bf16[32,1024]{1,0:T(8,128)(2,1)} %weight_hbm.1), channel_id=1, source_target_pairs={{0,32},{32,0},{1,33},{33,1},{2,34},{34,2},{3,35},{35,3},{4,36},{36... | collective-permute-start | bytes 196616 | tf_op jit(solution)/shard_map/ppermute | solution.py:219
  13.9 19.6 %all-to-all-start = ((bf16[8,256,128]{2,1,0:T(8,128)(2,1)}), bf16[8,256,128]{2,1,0:T(8,128)(2,1)S(1)}, u32[]{:S(2)}, u32[]{:S(2)}) async-start(bf16[8,256,128]{2,1,0:T(8,128)(2,1)} %get-tuple-element.11), calls=%async_computation | async-start | bytes 1048576 | tf_op jit(solution)/shard_map/all_to_all | solution.py:200
  34.8 23.0 %all-to-all-start.1 = ((bf16[16,16,128]{2,1,0:T(8,128)(2,1)}), bf16[16,16,128]{2,1,0:T(8,128)(2,1)S(1)}, u32[]{:S(2)}, u32[]{:S(2)}) async-start(bf16[16,16,128]{2,1,0:T(8,128)(2,1)} %get-tuple-element.12), calls=%async_computation.1 | async-start | bytes 131072 | tf_op jit(solution)/shard_map/all_to_all | solution.py:200
Sparse Core Ops, SparseCore 0:
  14.0 61.1 all-gather.1

commit v5 on v4

--- a/solution.py
+++ b/solution.py
@@ -26,18 +26,30 @@
     value_hbm,
     query_hbm,
     weight_hbm,
+    scale_hbm,
+    res_hbm,
     out_ref,
     pair_hbm,
     key_ref,
     value_ref,
     query_ref,
     weight_ref,
+    scale_ref,
+    res_ref,
+    prod_ref,
     sems,
 ):
     loads = [
         pltpu.make_async_copy(src, dst, sems.at[i])
         for i, (src, dst) in enumerate(
-            ((key_hbm, key_ref), (value_hbm, value_ref), (query_hbm, query_ref), (weight_hbm, weight_ref))
+            (
+                (key_hbm, key_ref),
+                (value_hbm, value_ref),
+                (query_hbm, query_ref),
+                (weight_hbm, weight_ref),
+                (scale_hbm, scale_ref),
+                (res_hbm, res_ref),
+            )
         )
     ]
     for load in loads:
@@ -46,46 +58,45 @@
         load.wait()
     rows = weight_hbm.shape[0]
     half = pair_hbm.at[pl.ds(pl.multiple_of(near_ref[0] * rows, rows), rows)]
-    store = pltpu.make_async_copy(weight_ref, half, sems.at[4])
+    store = pltpu.make_async_copy(weight_ref, half, sems.at[6])
     store.start()
     tokens = key_ref.shape[0]
     parts, _, lanes = out_ref.shape
     for part in range(parts):
         cols = slice(part * lanes, (part + 1) * lanes)
         product = key_ref[:, cols].astype(F32) * value_ref[:, cols].astype(F32)
-        out_ref[part, :tokens] = product.astype(BF16)
-        out_ref[part, tokens:] = query_ref[:, cols]
-    store.wait()
-
-
-def states_kernel(slices_ref, scale_ref, res_ref, totals_ref, states_ref, prod_ref):
-    parts, tokens, lanes = prod_ref.shape
-    modes = scale_ref.shape[0]
-    prod_ref[...] = slices_ref[:, :tokens].astype(F32)
+        product = product.astype(BF16)
+        prod_ref[:, cols] = product.astype(F32)
+        out_ref[part, :tokens] = product
+        out_ref[part, tokens : 2 * tokens] = query_ref[:, cols]
     scale = scale_ref[...]
     decay = jnp.exp(scale * (-1.0 / SEQ))
-    gain = gain_of(scale, res_ref[...])
-
-    def step(t, states):
-        return tuple(
-            state * decay + prod_ref[part, pl.ds(t, 1), :] for part, state in enumerate(states)
-        )
-
-    zero = jnp.zeros((modes, lanes), F32)
-    states = lax.fori_loop(0, tokens, step, (zero,) * parts, unroll=8)
-    decay = jnp.exp(scale * (-1.0 / 128))
-    total = zero
-    for part in range(parts):
-        state = states[part] * gain
-        states_ref[part] = state
-        total = total * decay + state
+
+    def step(t, state):
+        return state * decay + prod_ref[pl.ds(t, 1), :]
+
+    state = lax.fori_loop(0, tokens, step, jnp.zeros(scale.shape, F32), unroll=8)
+    state = (state * gain_of(scale, res_ref[...])).astype(BF16)
+    for part in range(parts):
+        out_ref[part, 2 * tokens :] = state[:, part * lanes : (part + 1) * lanes]
+    store.wait()
+
+
+def states_kernel(slices_ref, scale_ref, totals_ref, after_ref):
+    modes, lanes = scale_ref.shape
+    parts, rows, _ = slices_ref.shape
+    decay = jnp.exp(scale_ref[...] * (-1.0 / 128))
+    total = jnp.zeros((modes, lanes), F32)
+    for part in range(parts):
+        total = total * decay + slices_ref[part, rows - modes :].astype(F32)
+    after_ref[...] = total[: after_ref.shape[0]]
     total = total.astype(BF16)
     for copy in range(totals_ref.shape[0]):
         totals_ref[copy] = total
 
 
 def local_kernel(
-    slices_ref, states_ref, scale_ref, res_ref, skip_ref, base_ref, powers_ref, prod_ref
+    slices_ref, after_ref, scale_ref, res_ref, skip_ref, base_ref, powers_ref, prod_ref
 ):
     parts, tokens, lanes = prod_ref.shape
     modes = scale_ref.shape[0]
@@ -96,7 +107,7 @@
     leap = jnp.exp(scale * (-1.0 / 128))
     starts = [jnp.zeros((modes, lanes), F32)]
     for part in range(parts - 1):
-        starts.append(starts[-1] * leap + states_ref[part])
+        starts.append(starts[-1] * leap + slices_ref[part, 2 * tokens :].astype(F32))
 
     def step(t, states):
         fresh = []
@@ -129,7 +140,7 @@
         conv = base_ref[part]
         for mode in range(modes):
             conv = conv + powers_ref[mode] * carry[mode : mode + 1, :]
-        gated = (slices_ref[part, tokens:].astype(F32) * conv).astype(BF16)
+        gated = (slices_ref[part, tokens : 2 * tokens].astype(F32) * conv).astype(BF16)
         for row in range(4):
             out_ref[2 * row + part % 2, part // 2] = gated
         carry = carry * leap
@@ -209,10 +220,19 @@
     near = z.reshape(1) % 2
     slices, half = call(
         product_kernel,
-        [arr(8, 2 * tokens, lanes), arr(64, width)],
-        (near, key, value, query, out_weight),
-        specs=[SMEM] + [HBM] * 4,
-        scratch=[load, load, load, pltpu.VMEM((32, width), BF16), pltpu.SemaphoreType.DMA((5,))],
+        [arr(8, 2 * tokens + modes, lanes), arr(64, width)],
+        (near, key, value, query, out_weight, scale, residues),
+        specs=[SMEM] + [HBM] * 6,
+        scratch=[
+            load,
+            load,
+            load,
+            pltpu.VMEM((32, width), BF16),
+            pltpu.VMEM((modes, width), F32),
+            pltpu.VMEM((modes, width), F32),
+            pltpu.VMEM((tokens, width), F32),
+            pltpu.SemaphoreType.DMA((7,)),
+        ],
         limit=62,
         cost=pl.CostEstimate(flops=2_000_000, bytes_accessed=4_000_000, transcendentals=0),
     )
@@ -225,18 +245,16 @@
         lax.dynamic_slice_in_dim(a, own, lanes, 1) for a in (scale, residues, skip.reshape(1, width))
     )
     work = pltpu.VMEM((8, tokens, lanes), F32)
-    totals, states = call(
+    totals, after = call(
         states_kernel,
-        [arr(16, modes, lanes), arr(8, modes, lanes, dtype=F32)],
-        (slices, scale, residues),
-        scratch=[work],
-        cost=pl.CostEstimate(flops=20_000_000, bytes_accessed=2_000_000, transcendentals=0),
+        [arr(16, modes, lanes), arr(8, lanes, dtype=F32)],
+        (slices, scale),
     )
     totals = exchange(totals, PLANES)
     base, powers = call(
         local_kernel,
         [arr(8, tokens, lanes, dtype=F32), arr(modes, tokens, lanes, dtype=F32)],
-        (slices, states, scale, residues, skip),
+        (slices, after, scale, residues, skip),
         scratch=[work],
         cost=pl.CostEstimate(flops=20_000_000, bytes_accessed=2_000_000, transcendentals=300_000),
     )

time: 110 us -> 111 us (level)
  blocking collectives: 40 us -> 42.8 us
    all_to_all x2, blocking collectives: 40 us -> 42.8 us  [exchange(): return lax.all_to_all(pieces, axes, split_axis=0, concat_axis=0, tiled=True)]
where the time goes in v5:
time: 111 us
  blocking collectives  42.8 us (39%)
  starting transfers between devices  24.3 us (22%)
  waiting for transfers between devices  18.4 us (17%)
  between operations  13.5 us (12%)
  Pallas kernels  10.2 us (9%)
  local copies, waits for them, and re-layouts  1.44 us (1%)
    all_to_all x2, blocking collectives, exchange(): return lax.all_to_all(pieces, axes, split_axis=0, concat_axis=0, tiled=True)  42.8 us
    all_to_all x2, starting transfers between devices, exchange(): return lax.all_to_all(pieces, axes, split_axis=0, concat_axis=0, tiled=True)  19.8 us
    all_to_all x2, waiting for transfers between devices, exchange(): return lax.all_to_all(pieces, axes, split_axis=0, concat_axis=0, tiled=True)  18.4 us
    pallas_call x6, Pallas kernels, call(): pl.pallas_call(kernel, out_shape=outs, in_specs=specs or [VMEM] * len(inp...  10.2 us
    ppermute x1, starting transfers between devices, body(): other = lax.ppermute(out_weight, 'zq', [(0, 1), (1, 0)])  4.49 us
  transfers between devices with their start and end apart: 4, of which 2 were waited for; matrix products, arithmetic and copies ran while one was open for 1% of the time, Pallas kernels for 6%

profile of v5, /device:TPU:1, one launch (start us, length us, event | category | flops | bytes accessed | tf_op | source)
XLA Modules:
  0.0 110.6 jit_solution(11089898684915474362)
XLA Ops:
  6.5 0.0 copy-start
  6.5 0.0 all-gather.2.cloned.1.call-start
  6.5 4.5 %collective-permute-start = (bf16[32,1024]{1,0:T(8,128)(2,1)}, bf16[32,1024]{1,0:T(8,128)(2,1)S(1)}, u32[]{:S(2)}, u32[]{:S(2)}) collective-permute-start(bf16[32,1024]{1,0:T(8,128)(2,1)} %weight_hbm.1), channel_id=1, source_target_pairs={{0,32},{32,0},{1,33},{33,1},{2,34},{34,2},{3,35},{35,3},{4,36},{36... | collective-permute-start | bytes 196616 | tf_op jit(solution)/shard_map/ppermute | solution.py:239
  11.1 3.0 %shard_map.73 = (bf16[8,272,128]{2,1,0:T(8,128)(2,1)}, bf16[64,1024]{1,0:T(8,128)(2,1)}) custom-call(s32[1]{0:T(128)S(6)} %select_n.21.near_ref, bf16[128,1024]{1,0:T(8,128)(2,1)} %key_hbm.1, bf16[128,1024]{1,0:T(8,128)(2,1)} %value_hbm.1, bf16[128,1024]{1,0:T(8,128)(2,1)} %query_hbm.1, bf16[32,1024]{1,0:T(8,128)(2,1)} %weight_hbm.1, f32[16,1024]{1,0:T(8,128)} %scale_hbm.1, ...), custom_call_target="tpu_custom_call" | custom-call | flops 2000000 | bytes 4000000 | tf_op jit(solution)/shard_map/pallas_call | solution.py:195
  14.1 0.0 collective-permute-done
  14.1 0.6 constant_dynamic-update-slice_fusion
  14.8 0.0 all-gather.2.cloned.1.call-update
  14.8 9.2 %all-to-all-start = ((bf16[8,272,128]{2,1,0:T(8,128)(2,1)}), bf16[8,272,128]{2,1,0:T(8,128)(2,1)S(1)}, u32[]{:S(2)}, u32[]{:S(2)}) async-start(bf16[8,272,128]{2,1,0:T(8,128)(2,1)} %get-tuple-element.11), calls=%async_computation | async-start | bytes 1114112 | tf_op jit(solution)/shard_map/all_to_all | solution.py:211
  24.0 0.7 constant_dynamic-slice_fusion
  24.7 9.1 %all-to-all-done.slices_ref = bf16[8,272,128]{2,1,0:T(8,128)(2,1)S(1)} async-done(((bf16[8,272,128]{2,1,0:T(8,128)(2,1)}), bf16[8,272,128]{2,1,0:T(8,128)(2,1)S(1)}, u32[]{:S(2)}, u32[]{:S(2)}) %all-to-all-start) | async-done | bytes 557088 | tf_op jit(solution)/shard_map/all_to_all | solution.py:211
  33.9 0.7 shard_map.74
  34.5 10.6 %all-to-all-start.1 = ((bf16[16,16,128]{2,1,0:T(8,128)(2,1)}), bf16[16,16,128]{2,1,0:T(8,128)(2,1)S(1)}, u32[]{:S(2)}, u32[]{:S(2)}) async-start(bf16[16,16,128]{2,1,0:T(8,128)(2,1)} %get-tuple-element.12), calls=%async_computation.1 | async-start | bytes 131072 | tf_op jit(solution)/shard_map/all_to_all | solution.py:211
  45.1 0.0 copy-done
  45.1 0.1 dynamic-slice_bitcast_fusion.skip_ref
  45.2 2.2 %shard_map.75 = (f32[8,128,128]{2,1,0:T(8,128)S(1)}, f32[16,128,128]{2,1,0:T(8,128)S(1)}) custom-call(bf16[8,272,128]{2,1,0:T(8,128)(2,1)S(1)} %all-to-all-done.slices_ref, f32[8,128]{1,0:T(8,128)S(1)} %get-tuple-element.13.after_ref, f32[16,128]{1,0:T(8,128)S(1)} %get-tuple-element.18.scale_ref, f32[16,128]{1,0:T(8,128)S(1)} %get-tuple-element.17.res_ref, ...), custom_call_target="tpu_custom_call" | custom-call | flops 20000000 | bytes 2000000 | tf_op jit(solution)/shard_map/pallas_call | solution.py:195
  47.4 9.2 %all-to-all-done.1.totals_ref = bf16[16,16,128]{2,1,0:T(8,128)(2,1)S(1)} async-done(((bf16[16,16,128]{2,1,0:T(8,128)(2,1)}), bf16[16,16,128]{2,1,0:T(8,128)(2,1)S(1)}, u32[]{:S(2)}, u32[]{:S(2)}) %all-to-all-start.1) | async-done | bytes 65568 | tf_op jit(solution)/shard_map/all_to_all | solution.py:211
  56.6 0.7 shard_map.76
  57.3 21.0 %all_to_all.20.gated_ref = bf16[8,4,128,128]{3,2,1,0:T(8,128)(2,1)S(1)} all-to-all(bf16[8,4,128,128]{3,2,1,0:T(8,128)(2,1)S(1)} %shard_map.76), channel_id=1, replica_groups=mesh['zp'=8,'zq'=2,'y'=4,'core'=2,'x'=4] {'y','core'}, dimensions={0} | all-to-all | bytes 2097152 | tf_op jit(solution)/shard_map/all_to_all | solution.py:211
  78.2 0.0 all-gather.2.cloned.1.call-done.weight_hbm
  78.2 2.7 %shard_map.77 = bf16[16,128,256]{2,1,0:T(8,128)(2,1)S(1)} custom-call(bf16[8,4,128,128]{3,2,1,0:T(8,128)(2,1)S(1)} %all_to_all.20.gated_ref, bf16[1024,1024]{1,0:T(8,128)(2,1)} %all-gather.2.cloned.1.call-done.weight_hbm), custom_call_target="tpu_custom_call" | custom-call | tf_op jit(solution)/shard_map/pallas_call | solution.py:195
  81.0 21.8 %all_to_all.21.pieces_ref = bf16[16,128,256]{2,1,0:T(8,128)(2,1)S(1)} all-to-all(bf16[16,128,256]{2,1,0:T(8,128)(2,1)S(1)} %shard_map.77), channel_id=1, replica_groups=mesh['zp'=8,'zq'=2,'y'=4,'core'=2,'x'=4] {'y','x'}, dimensions={0} | all-to-all | bytes 2097152 | tf_op jit(solution)/shard_map/all_to_all | solution.py:211
  102.8 0.9 shard_map.78
Async XLA Ops:
  6.5 38.5 %copy-start = (f32[1024]{0:T(1024)S(1)}, f32[1024]{0:T(1024)}, u32[]{:S(2)}) copy-start(f32[1024]{0:T(1024)} %param.12) | copy-start | bytes 12292
  6.5 71.7 %all-gather.2.cloned.1.call-start = ((), (), s32[]{:S(2)}) async-start(), calls=%async_computation.4 | async-start | bytes 2228224 | tf_op jit(solution)/shard_map/all_gather | solution.py:241
  6.5 7.6 %collective-permute-start = (bf16[32,1024]{1,0:T(8,128)(2,1)}, bf16[32,1024]{1,0:T(8,128)(2,1)S(1)}, u32[]{:S(2)}, u32[]{:S(2)}) collective-permute-start(bf16[32,1024]{1,0:T(8,128)(2,1)} %weight_hbm.1), channel_id=1, source_target_pairs={{0,32},{32,0},{1,33},{33,1},{2,34},{34,2},{3,35},{35,3},{4,36},{36... | collective-permute-start | bytes 196616 | tf_op jit(solution)/shard_map/ppermute | solution.py:239
  14.8 19.1 %all-to-all-start = ((bf16[8,272,128]{2,1,0:T(8,128)(2,1)}), bf16[8,272,128]{2,1,0:T(8,128)(2,1)S(1)}, u32[]{:S(2)}, u32[]{:S(2)}) async-start(bf16[8,272,128]{2,1,0:T(8,128)(2,1)} %get-tuple-element.11), calls=%async_computation | async-start | bytes 1114112 | tf_op jit(solution)/shard_map/all_to_all | solution.py:211
  34.5 22.1 %all-to-all-start.1 = ((bf16[16,16,128]{2,1,0:T(8,128)(2,1)}), bf16[16,16,128]{2,1,0:T(8,128)(2,1)S(1)}, u32[]{:S(2)}, u32[]{:S(2)}) async-start(bf16[16,16,128]{2,1,0:T(8,128)(2,1)} %get-tuple-element.12), calls=%async_computation.1 | async-start | bytes 131072 | tf_op jit(solution)/shard_map/all_to_all | solution.py:211
Sparse Core Ops, SparseCore 0:
  14.9 59.6 all-gather.1

commit v6 on v4

--- a/solution.py
+++ b/solution.py
@@ -12,8 +12,12 @@
 VMEM = pl.BlockSpec(memory_space=pltpu.VMEM)
 HBM = pl.BlockSpec(memory_space=pltpu.HBM)
 SMEM = pl.BlockSpec(memory_space=pltpu.SMEM)
-NEAR = ("y", "core")
+NEAR = ("core", "y")
 PLANES = ("zp", "zq")
+
+
+def member(part):
+    return 4 * (part % 2) + part // 2
 
 
 def gain_of(scale, residues):
@@ -61,7 +65,8 @@
 def states_kernel(slices_ref, scale_ref, res_ref, totals_ref, states_ref, prod_ref):
     parts, tokens, lanes = prod_ref.shape
     modes = scale_ref.shape[0]
-    prod_ref[...] = slices_ref[:, :tokens].astype(F32)
+    for part in range(parts):
+        prod_ref[part] = slices_ref[member(part), :tokens].astype(F32)
     scale = scale_ref[...]
     decay = jnp.exp(scale * (-1.0 / SEQ))
     gain = gain_of(scale, res_ref[...])
@@ -89,7 +94,8 @@
 ):
     parts, tokens, lanes = prod_ref.shape
     modes = scale_ref.shape[0]
-    prod_ref[...] = slices_ref[:, :tokens].astype(F32)
+    for part in range(parts):
+        prod_ref[part] = slices_ref[member(part), :tokens].astype(F32)
     scale = scale_ref[...]
     decay = jnp.exp(scale * (-1.0 / SEQ))
     gain = gain_of(scale, res_ref[...])
@@ -129,9 +135,9 @@
         conv = base_ref[part]
         for mode in range(modes):
             conv = conv + powers_ref[mode] * carry[mode : mode + 1, :]
-        gated = (slices_ref[part, tokens:].astype(F32) * conv).astype(BF16)
+        gated = (slices_ref[member(part), tokens:].astype(F32) * conv).astype(BF16)
         for row in range(4):
-            out_ref[2 * row + part % 2, part // 2] = gated
+            out_ref[4 * (part % 2) + row, part // 2] = gated
         carry = carry * leap
 
 

time: 110 us -> 110 us (level)
  no operation moved by 1% of the time
where the time goes in v6:
time: 110 us; the launch traced here: 109 us
  blocking collectives  40.1 us (36%)
  starting transfers between devices  25.2 us (23%)
  waiting for transfers between devices  18.6 us (17%)
  between operations  13.5 us (12%)
  Pallas kernels  9.95 us (9%)
  local copies, waits for them, and re-layouts  1.44 us (1%)
    all_to_all x2, blocking collectives, exchange(): return lax.all_to_all(pieces, axes, split_axis=0, concat_axis=0, tiled=True)  40.1 us
    all_to_all x2, starting transfers between devices, exchange(): return lax.all_to_all(pieces, axes, split_axis=0, concat_axis=0, tiled=True)  20.7 us
    all_to_all x2, waiting for transfers between devices, exchange(): return lax.all_to_all(pieces, axes, split_axis=0, concat_axis=0, tiled=True)  18.5 us
    pallas_call x6, Pallas kernels, call(): pl.pallas_call(kernel, out_shape=outs, in_specs=specs or [VMEM] * len(inp...  9.95 us
    ppermute x1, starting transfers between devices, body(): other = lax.ppermute(out_weight, 'zq', [(0, 1), (1, 0)])  4.49 us
  transfers between devices with their start and end apart: 4, of which 2 were waited for; matrix products, arithmetic and copies ran while one was open for 1% of the time, Pallas kernels for 6%

profile of v6, /device:TPU:1, one launch (start us, length us, event | category | flops | bytes accessed | tf_op | source)
XLA Modules:
  0.0 108.7 jit_solution(15899887188486133128)
XLA Ops:
  6.5 0.0 copy-start
  6.5 0.0 all-gather.2.cloned.1.call-start
  6.5 4.5 %collective-permute-start = (bf16[32,1024]{1,0:T(8,128)(2,1)}, bf16[32,1024]{1,0:T(8,128)(2,1)S(1)}, u32[]{:S(2)}, u32[]{:S(2)}) collective-permute-start(bf16[32,1024]{1,0:T(8,128)(2,1)} %weight_hbm.1), channel_id=1, source_target_pairs={{0,32},{32,0},{1,33},{33,1},{2,34},{34,2},{3,35},{35,3},{4,36},{36... | collective-permute-start | bytes 196616 | tf_op jit(solution)/shard_map/ppermute | solution.py:225
  11.1 2.1 %shard_map.73 = (bf16[8,256,128]{2,1,0:T(8,128)(2,1)}, bf16[64,1024]{1,0:T(8,128)(2,1)}) custom-call(s32[1]{0:T(128)S(6)} %select_n.21.near_ref, bf16[128,1024]{1,0:T(8,128)(2,1)} %key_hbm.1, bf16[128,1024]{1,0:T(8,128)(2,1)} %value_hbm.1, bf16[128,1024]{1,0:T(8,128)(2,1)} %query_hbm.1, bf16[32,1024]{1,0:T(8,128)(2,1)} %weight_hbm.1), custom_call_target="tpu_custom_call" | custom-call | flops 2000000 | bytes 4000000 | tf_op jit(solution)/shard_map/pallas_call | solution.py:190
  13.2 0.0 collective-permute-done
  13.2 0.6 constant_dynamic-update-slice_fusion
  13.9 0.0 all-gather.2.cloned.1.call-update
  13.9 10.1 %all-to-all-start = ((bf16[8,256,128]{2,1,0:T(8,128)(2,1)}), bf16[8,256,128]{2,1,0:T(8,128)(2,1)S(1)}, u32[]{:S(2)}, u32[]{:S(2)}) async-start(bf16[8,256,128]{2,1,0:T(8,128)(2,1)} %get-tuple-element.11), calls=%async_computation | async-start | bytes 1048576 | tf_op jit(solution)/shard_map/all_to_all | solution.py:206
  24.0 0.7 constant_dynamic-slice_fusion
  24.7 8.7 %all-to-all-done.slices_ref = bf16[8,256,128]{2,1,0:T(8,128)(2,1)S(1)} async-done(((bf16[8,256,128]{2,1,0:T(8,128)(2,1)}), bf16[8,256,128]{2,1,0:T(8,128)(2,1)S(1)}, u32[]{:S(2)}, u32[]{:S(2)}) %all-to-all-start) | async-done | bytes 524320 | tf_op jit(solution)/shard_map/all_to_all | solution.py:206
  33.4 1.3 %shard_map.74 = (bf16[16,16,128]{2,1,0:T(8,128)(2,1)}, f32[8,16,128]{2,1,0:T(8,128)S(1)}) custom-call(bf16[8,256,128]{2,1,0:T(8,128)(2,1)S(1)} %all-to-all-done.slices_ref, f32[16,128]{1,0:T(8,128)S(1)} %get-tuple-element.18.scale_ref, f32[16,128]{1,0:T(8,128)S(1)} %get-tuple-element.17.res_ref), custom_call_target="tpu_custom_call" | custom-call | flops 20000000 | bytes 2000000 | tf_op jit(solution)/shard_map/pallas_call | solution.py:190
  34.6 10.6 %all-to-all-start.1 = ((bf16[16,16,128]{2,1,0:T(8,128)(2,1)}), bf16[16,16,128]{2,1,0:T(8,128)(2,1)S(1)}, u32[]{:S(2)}, u32[]{:S(2)}) async-start(bf16[16,16,128]{2,1,0:T(8,128)(2,1)} %get-tuple-element.12), calls=%async_computation.1 | async-start | bytes 131072 | tf_op jit(solution)/shard_map/all_to_all | solution.py:206
  45.2 0.0 copy-done
  45.3 0.1 dynamic-slice_bitcast_fusion.skip_ref
  45.3 2.2 %shard_map.75 = (f32[8,128,128]{2,1,0:T(8,128)S(1)}, f32[16,128,128]{2,1,0:T(8,128)S(1)}) custom-call(bf16[8,256,128]{2,1,0:T(8,128)(2,1)S(1)} %all-to-all-done.slices_ref, f32[8,16,128]{2,1,0:T(8,128)S(1)} %get-tuple-element.13.states_ref, f32[16,128]{1,0:T(8,128)S(1)} %get-tuple-element.18.scale_ref, f32[16,128]{1,0:T(8,128)S(1)} %get-tuple-element.17.res_ref, ...), custom_call_target="tpu_custom_call" | custom-call | flops 20000000 | bytes 2000000 | tf_op jit(solution)/shard_map/pallas_call | solution.py:190
  47.6 9.9 %all-to-all-done.1.totals_ref = bf16[16,16,128]{2,1,0:T(8,128)(2,1)S(1)} async-done(((bf16[16,16,128]{2,1,0:T(8,128)(2,1)}), bf16[16,16,128]{2,1,0:T(8,128)(2,1)S(1)}, u32[]{:S(2)}, u32[]{:S(2)}) %all-to-all-start.1) | async-done | bytes 65568 | tf_op jit(solution)/shard_map/all_to_all | solution.py:206
  57.4 0.7 shard_map.76
  58.1 19.8 %all_to_all.20.gated_ref = bf16[8,4,128,128]{3,2,1,0:T(8,128)(2,1)S(1)} all-to-all(bf16[8,4,128,128]{3,2,1,0:T(8,128)(2,1)S(1)} %shard_map.76), channel_id=1, replica_groups=mesh['zp'=8,'zq'=2,'y'=4,'core'=2,'x'=4] {'core','y'}, dimensions={0} | all-to-all | bytes 2097152 | tf_op jit(solution)/shard_map/all_to_all | solution.py:206
  77.9 0.0 all-gather.2.cloned.1.call-done.weight_hbm
  77.9 2.7 %shard_map.77 = bf16[16,128,256]{2,1,0:T(8,128)(2,1)S(1)} custom-call(bf16[8,4,128,128]{3,2,1,0:T(8,128)(2,1)S(1)} %all_to_all.20.gated_ref, bf16[1024,1024]{1,0:T(8,128)(2,1)} %all-gather.2.cloned.1.call-done.weight_hbm), custom_call_target="tpu_custom_call" | custom-call | tf_op jit(solution)/shard_map/pallas_call | solution.py:190
  80.6 20.3 %all_to_all.21.pieces_ref = bf16[16,128,256]{2,1,0:T(8,128)(2,1)S(1)} all-to-all(bf16[16,128,256]{2,1,0:T(8,128)(2,1)S(1)} %shard_map.77), channel_id=1, replica_groups=mesh['zp'=8,'zq'=2,'y'=4,'core'=2,'x'=4] {'y','x'}, dimensions={0} | all-to-all | bytes 2097152 | tf_op jit(solution)/shard_map/all_to_all | solution.py:206
  100.9 0.9 shard_map.78
Async XLA Ops:
  6.5 38.7 %copy-start = (f32[1024]{0:T(1024)S(1)}, f32[1024]{0:T(1024)}, u32[]{:S(2)}) copy-start(f32[1024]{0:T(1024)} %param.12) | copy-start | bytes 12292
  6.5 71.4 %all-gather.2.cloned.1.call-start = ((), (), s32[]{:S(2)}) async-start(), calls=%async_computation.4 | async-start | bytes 2228224 | tf_op jit(solution)/shard_map/all_gather | solution.py:227
  6.5 6.7 %collective-permute-start = (bf16[32,1024]{1,0:T(8,128)(2,1)}, bf16[32,1024]{1,0:T(8,128)(2,1)S(1)}, u32[]{:S(2)}, u32[]{:S(2)}) collective-permute-start(bf16[32,1024]{1,0:T(8,128)(2,1)} %weight_hbm.1), channel_id=1, source_target_pairs={{0,32},{32,0},{1,33},{33,1},{2,34},{34,2},{3,35},{35,3},{4,36},{36... | collective-permute-start | bytes 196616 | tf_op jit(solution)/shard_map/ppermute | solution.py:225
  13.9 19.5 %all-to-all-start = ((bf16[8,256,128]{2,1,0:T(8,128)(2,1)}), bf16[8,256,128]{2,1,0:T(8,128)(2,1)S(1)}, u32[]{:S(2)}, u32[]{:S(2)}) async-start(bf16[8,256,128]{2,1,0:T(8,128)(2,1)} %get-tuple-element.11), calls=%async_computation | async-start | bytes 1048576 | tf_op jit(solution)/shard_map/all_to_all | solution.py:206
  34.6 22.8 %all-to-all-start.1 = ((bf16[16,16,128]{2,1,0:T(8,128)(2,1)}), bf16[16,16,128]{2,1,0:T(8,128)(2,1)S(1)}, u32[]{:S(2)}, u32[]{:S(2)}) async-start(bf16[16,16,128]{2,1,0:T(8,128)(2,1)} %get-tuple-element.12), calls=%async_computation.1 | async-start | bytes 131072 | tf_op jit(solution)/shard_map/all_to_all | solution.py:206
Sparse Core Ops, SparseCore 0:
  14.0 60.8 all-gather.1

commit v7 on v6

--- a/solution.py
+++ b/solution.py
@@ -169,16 +169,16 @@
         ).astype(BF16)
         for i, quarter in enumerate(quarters):
             for block in range(blocks):
-                out_ref[block * 4 + quarter] = terms[
+                out_ref[quarter * 4 + block] = terms[
                     block * tokens : (block + 1) * tokens, 256 * i : 256 * i + 256
                 ]
 
 
 def sum_kernel(pieces_ref, out_ref):
     for row in range(4):
-        total = pieces_ref[row * 4].astype(F32)
+        total = pieces_ref[row].astype(F32)
         for owner in range(1, 4):
-            total = total + pieces_ref[row * 4 + owner].astype(F32)
+            total = total + pieces_ref[owner * 4 + row].astype(F32)
         total = total.astype(BF16)
         for plane in range(4):
             start = plane * 256 + row * 64
@@ -265,7 +265,7 @@
         ],
         limit=50.5,
     )
-    terms = exchange(terms, ("y", "x"))
+    terms = exchange(terms, ("x", "y"))
     return call(sum_kernel, arr(tokens, width), (terms,))
 
 

time: 110 us -> 110 us (level)
  the two profiles are of different devices: /device:TPU:1 before, /device:TPU:32 now
where the time goes in v7:
time: 110 us; the launch traced here: 109 us
  blocking collectives  40.6 us (37%)
  starting transfers between devices  23.8 us (22%)
  waiting for transfers between devices  19.9 us (18%)
  between operations  13.5 us (12%)
  Pallas kernels  9.95 us (9%)
  local copies, waits for them, and re-layouts  1.44 us (1%)
    all_to_all x2, blocking collectives, exchange(): return lax.all_to_all(pieces, axes, split_axis=0, concat_axis=0, tiled=True)  40.6 us
    all_to_all x2, waiting for transfers between devices, exchange(): return lax.all_to_all(pieces, axes, split_axis=0, concat_axis=0, tiled=True)  19.6 us
    all_to_all x2, starting transfers between devices, exchange(): return lax.all_to_all(pieces, axes, split_axis=0, concat_axis=0, tiled=True)  16.3 us
    pallas_call x6, Pallas kernels, call(): pl.pallas_call(kernel, out_shape=outs, in_specs=specs or [VMEM] * len(inp...  9.95 us
    ppermute x1, starting transfers between devices, body(): other = lax.ppermute(out_weight, 'zq', [(0, 1), (1, 0)])  7.51 us
  transfers between devices with their start and end apart: 4, of which 3 were waited for; matrix products, arithmetic and copies ran while one was open for 1% of the time, Pallas kernels for 6%

profile of v7, /device:TPU:32, one launch (start us, length us, event | category | flops | bytes accessed | tf_op | source)
XLA Modules:
  0.0 109.2 jit_solution(14577345312207807450)
XLA Ops:
  6.5 0.0 copy-start
  6.5 0.0 all-gather.2.cloned.1.call-start
  6.5 7.5 %collective-permute-start = (bf16[32,1024]{1,0:T(8,128)(2,1)}, bf16[32,1024]{1,0:T(8,128)(2,1)S(1)}, u32[]{:S(2)}, u32[]{:S(2)}) collective-permute-start(bf16[32,1024]{1,0:T(8,128)(2,1)} %weight_hbm.1), channel_id=1, source_target_pairs={{0,32},{32,0},{1,33},{33,1},{2,34},{34,2},{3,35},{35,3},{4,36},{36... | collective-permute-start | bytes 196616 | tf_op jit(solution)/shard_map/ppermute | solution.py:225
  14.1 2.1 %shard_map.73 = (bf16[8,256,128]{2,1,0:T(8,128)(2,1)}, bf16[64,1024]{1,0:T(8,128)(2,1)}) custom-call(s32[1]{0:T(128)S(6)} %select_n.21.near_ref, bf16[128,1024]{1,0:T(8,128)(2,1)} %key_hbm.1, bf16[128,1024]{1,0:T(8,128)(2,1)} %value_hbm.1, bf16[128,1024]{1,0:T(8,128)(2,1)} %query_hbm.1, bf16[32,1024]{1,0:T(8,128)(2,1)} %weight_hbm.1), custom_call_target="tpu_custom_call" | custom-call | flops 2000000 | bytes 4000000 | tf_op jit(solution)/shard_map/pallas_call | solution.py:190
  16.2 0.3 collective-permute-done
  16.5 0.6 constant_dynamic-update-slice_fusion
  17.1 0.0 all-gather.2.cloned.1.call-update
  17.2 3.5 %all-to-all-start = ((bf16[8,256,128]{2,1,0:T(8,128)(2,1)}), bf16[8,256,128]{2,1,0:T(8,128)(2,1)S(1)}, u32[]{:S(2)}, u32[]{:S(2)}) async-start(bf16[8,256,128]{2,1,0:T(8,128)(2,1)} %get-tuple-element.11), calls=%async_computation | async-start | bytes 1048576 | tf_op jit(solution)/shard_map/all_to_all | solution.py:206
  20.7 0.7 constant_dynamic-slice_fusion
  21.4 8.9 %all-to-all-done.slices_ref = bf16[8,256,128]{2,1,0:T(8,128)(2,1)S(1)} async-done(((bf16[8,256,128]{2,1,0:T(8,128)(2,1)}), bf16[8,256,128]{2,1,0:T(8,128)(2,1)S(1)}, u32[]{:S(2)}, u32[]{:S(2)}) %all-to-all-start) | async-done | bytes 524320 | tf_op jit(solution)/shard_map/all_to_all | solution.py:206
  30.3 1.3 %shard_map.74 = (bf16[16,16,128]{2,1,0:T(8,128)(2,1)}, f32[8,16,128]{2,1,0:T(8,128)S(1)}) custom-call(bf16[8,256,128]{2,1,0:T(8,128)(2,1)S(1)} %all-to-all-done.slices_ref, f32[16,128]{1,0:T(8,128)S(1)} %get-tuple-element.18.scale_ref, f32[16,128]{1,0:T(8,128)S(1)} %get-tuple-element.17.res_ref), custom_call_target="tpu_custom_call" | custom-call | flops 20000000 | bytes 2000000 | tf_op jit(solution)/shard_map/pallas_call | solution.py:190
  31.6 12.8 %all-to-all-start.1 = ((bf16[16,16,128]{2,1,0:T(8,128)(2,1)}), bf16[16,16,128]{2,1,0:T(8,128)(2,1)S(1)}, u32[]{:S(2)}, u32[]{:S(2)}) async-start(bf16[16,16,128]{2,1,0:T(8,128)(2,1)} %get-tuple-element.12), calls=%async_computation.1 | async-start | bytes 131072 | tf_op jit(solution)/shard_map/all_to_all | solution.py:206
  44.4 0.0 copy-done
  44.4 0.1 dynamic-slice_bitcast_fusion.skip_ref
  44.5 2.2 %shard_map.75 = (f32[8,128,128]{2,1,0:T(8,128)S(1)}, f32[16,128,128]{2,1,0:T(8,128)S(1)}) custom-call(bf16[8,256,128]{2,1,0:T(8,128)(2,1)S(1)} %all-to-all-done.slices_ref, f32[8,16,128]{2,1,0:T(8,128)S(1)} %get-tuple-element.13.states_ref, f32[16,128]{1,0:T(8,128)S(1)} %get-tuple-element.18.scale_ref, f32[16,128]{1,0:T(8,128)S(1)} %get-tuple-element.17.res_ref, ...), custom_call_target="tpu_custom_call" | custom-call | flops 20000000 | bytes 2000000 | tf_op jit(solution)/shard_map/pallas_call | solution.py:190
  46.7 10.7 %all-to-all-done.1.totals_ref = bf16[16,16,128]{2,1,0:T(8,128)(2,1)S(1)} async-done(((bf16[16,16,128]{2,1,0:T(8,128)(2,1)}), bf16[16,16,128]{2,1,0:T(8,128)(2,1)S(1)}, u32[]{:S(2)}, u32[]{:S(2)}) %all-to-all-start.1) | async-done | bytes 65568 | tf_op jit(solution)/shard_map/all_to_all | solution.py:206
  57.4 0.7 shard_map.76
  58.1 18.2 %all_to_all.20.gated_ref = bf16[8,4,128,128]{3,2,1,0:T(8,128)(2,1)S(1)} all-to-all(bf16[8,4,128,128]{3,2,1,0:T(8,128)(2,1)S(1)} %shard_map.76), channel_id=1, replica_groups=mesh['zp'=8,'zq'=2,'y'=4,'core'=2,'x'=4] {'core','y'}, dimensions={0} | all-to-all | bytes 2097152 | tf_op jit(solution)/shard_map/all_to_all | solution.py:206
  76.3 0.0 all-gather.2.cloned.1.call-done.weight_hbm
  76.3 2.7 %shard_map.77 = bf16[16,128,256]{2,1,0:T(8,128)(2,1)S(1)} custom-call(bf16[8,4,128,128]{3,2,1,0:T(8,128)(2,1)S(1)} %all_to_all.20.gated_ref, bf16[1024,1024]{1,0:T(8,128)(2,1)} %all-gather.2.cloned.1.call-done.weight_hbm), custom_call_target="tpu_custom_call" | custom-call | tf_op jit(solution)/shard_map/pallas_call | solution.py:190
  79.0 22.4 %all_to_all.21.pieces_ref = bf16[16,128,256]{2,1,0:T(8,128)(2,1)S(1)} all-to-all(bf16[16,128,256]{2,1,0:T(8,128)(2,1)S(1)} %shard_map.77), channel_id=1, replica_groups=mesh['zp'=8,'zq'=2,'y'=4,'core'=2,'x'=4] {'x','y'}, dimensions={0} | all-to-all | bytes 2097152 | tf_op jit(solution)/shard_map/all_to_all | solution.py:206
  101.4 0.9 shard_map.78
Async XLA Ops:
  6.5 37.9 %copy-start = (f32[1024]{0:T(1024)S(1)}, f32[1024]{0:T(1024)}, u32[]{:S(2)}) copy-start(f32[1024]{0:T(1024)} %param.12) | copy-start | bytes 12292
  6.5 69.7 %all-gather.2.cloned.1.call-start = ((), (), s32[]{:S(2)}) async-start(), calls=%async_computation.4 | async-start | bytes 2228224 | tf_op jit(solution)/shard_map/all_gather | solution.py:227
  6.5 10.0 %collective-permute-start = (bf16[32,1024]{1,0:T(8,128)(2,1)}, bf16[32,1024]{1,0:T(8,128)(2,1)S(1)}, u32[]{:S(2)}, u32[]{:S(2)}) collective-permute-start(bf16[32,1024]{1,0:T(8,128)(2,1)} %weight_hbm.1), channel_id=1, source_target_pairs={{0,32},{32,0},{1,33},{33,1},{2,34},{34,2},{3,35},{35,3},{4,36},{36... | collective-permute-start | bytes 196616 | tf_op jit(solution)/shard_map/ppermute | solution.py:225
  17.2 13.2 %all-to-all-start = ((bf16[8,256,128]{2,1,0:T(8,128)(2,1)}), bf16[8,256,128]{2,1,0:T(8,128)(2,1)S(1)}, u32[]{:S(2)}, u32[]{:S(2)}) async-start(bf16[8,256,128]{2,1,0:T(8,128)(2,1)} %get-tuple-element.11), calls=%async_computation | async-start | bytes 1048576 | tf_op jit(solution)/shard_map/all_to_all | solution.py:206
  31.6 25.8 %all-to-all-start.1 = ((bf16[16,16,128]{2,1,0:T(8,128)(2,1)}), bf16[16,16,128]{2,1,0:T(8,128)(2,1)S(1)}, u32[]{:S(2)}, u32[]{:S(2)}) async-start(bf16[16,16,128]{2,1,0:T(8,128)(2,1)} %get-tuple-element.12), calls=%async_computation.1 | async-start | bytes 131072 | tf_op jit(solution)/shard_map/all_to_all | solution.py:206
Sparse Core Ops, SparseCore 0:
  17.3 54.1 all-gather.1

commit v8 on v6

--- a/solution.py
+++ b/solution.py
@@ -77,7 +77,7 @@
         )
 
     zero = jnp.zeros((modes, lanes), F32)
-    states = lax.fori_loop(0, tokens, step, (zero,) * parts, unroll=8)
+    states = lax.fori_loop(0, tokens, step, (zero,) * parts, unroll=16)
     decay = jnp.exp(scale * (-1.0 / 128))
     total = zero
     for part in range(parts):

time: 110 us -> 110 us (level)
  no operation moved by 1% of the time
where the time goes in v8:
time: 110 us; the launch traced here: 109 us
  blocking collectives  40.1 us (36%)
  starting transfers between devices  25.2 us (23%)
  waiting for transfers between devices  18.5 us (17%)
  between operations  13.5 us (12%)
  Pallas kernels  9.93 us (9%)
  local copies, waits for them, and re-layouts  1.44 us (1%)
    all_to_all x2, blocking collectives, exchange(): return lax.all_to_all(pieces, axes, split_axis=0, concat_axis=0, tiled=True)  40.1 us
    all_to_all x2, starting transfers between devices, exchange(): return lax.all_to_all(pieces, axes, split_axis=0, concat_axis=0, tiled=True)  20.7 us
    all_to_all x2, waiting for transfers between devices, exchange(): return lax.all_to_all(pieces, axes, split_axis=0, concat_axis=0, tiled=True)  18.5 us
    pallas_call x6, Pallas kernels, call(): pl.pallas_call(kernel, out_shape=outs, in_specs=specs or [VMEM] * len(inp...  9.93 us
    ppermute x1, starting transfers between devices, body(): other = lax.ppermute(out_weight, 'zq', [(0, 1), (1, 0)])  4.49 us
  transfers between devices with their start and end apart: 4, of which 2 were waited for; matrix products, arithmetic and copies ran while one was open for 1% of the time, Pallas kernels for 6%

profile of v8, /device:TPU:1, one launch (start us, length us, event | category | flops | bytes accessed | tf_op | source)
XLA Modules:
  0.0 108.6 jit_solution(419624010990885932)
XLA Ops:
  6.5 0.0 copy-start
  6.5 0.0 all-gather.2.cloned.1.call-start
  6.5 4.5 %collective-permute-start = (bf16[32,1024]{1,0:T(8,128)(2,1)}, bf16[32,1024]{1,0:T(8,128)(2,1)S(1)}, u32[]{:S(2)}, u32[]{:S(2)}) collective-permute-start(bf16[32,1024]{1,0:T(8,128)(2,1)} %weight_hbm.1), channel_id=1, source_target_pairs={{0,32},{32,0},{1,33},{33,1},{2,34},{34,2},{3,35},{35,3},{4,36},{36... | collective-permute-start | bytes 196616 | tf_op jit(solution)/shard_map/ppermute | solution.py:225
  11.1 2.1 %shard_map.73 = (bf16[8,256,128]{2,1,0:T(8,128)(2,1)}, bf16[64,1024]{1,0:T(8,128)(2,1)}) custom-call(s32[1]{0:T(128)S(6)} %select_n.21.near_ref, bf16[128,1024]{1,0:T(8,128)(2,1)} %key_hbm.1, bf16[128,1024]{1,0:T(8,128)(2,1)} %value_hbm.1, bf16[128,1024]{1,0:T(8,128)(2,1)} %query_hbm.1, bf16[32,1024]{1,0:T(8,128)(2,1)} %weight_hbm.1), custom_call_target="tpu_custom_call" | custom-call | flops 2000000 | bytes 4000000 | tf_op jit(solution)/shard_map/pallas_call | solution.py:190
  13.2 0.0 collective-permute-done
  13.2 0.6 constant_dynamic-update-slice_fusion
  13.9 0.0 all-gather.2.cloned.1.call-update
  13.9 10.1 %all-to-all-start = ((bf16[8,256,128]{2,1,0:T(8,128)(2,1)}), bf16[8,256,128]{2,1,0:T(8,128)(2,1)S(1)}, u32[]{:S(2)}, u32[]{:S(2)}) async-start(bf16[8,256,128]{2,1,0:T(8,128)(2,1)} %get-tuple-element.11), calls=%async_computation | async-start | bytes 1048576 | tf_op jit(solution)/shard_map/all_to_all | solution.py:206
  24.0 0.7 constant_dynamic-slice_fusion
  24.7 8.7 %all-to-all-done.slices_ref = bf16[8,256,128]{2,1,0:T(8,128)(2,1)S(1)} async-done(((bf16[8,256,128]{2,1,0:T(8,128)(2,1)}), bf16[8,256,128]{2,1,0:T(8,128)(2,1)S(1)}, u32[]{:S(2)}, u32[]{:S(2)}) %all-to-all-start) | async-done | bytes 524320 | tf_op jit(solution)/shard_map/all_to_all | solution.py:206
  33.4 1.3 %shard_map.74 = (bf16[16,16,128]{2,1,0:T(8,128)(2,1)}, f32[8,16,128]{2,1,0:T(8,128)S(1)}) custom-call(bf16[8,256,128]{2,1,0:T(8,128)(2,1)S(1)} %all-to-all-done.slices_ref, f32[16,128]{1,0:T(8,128)S(1)} %get-tuple-element.18.scale_ref, f32[16,128]{1,0:T(8,128)S(1)} %get-tuple-element.17.res_ref), custom_call_target="tpu_custom_call" | custom-call | flops 20000000 | bytes 2000000 | tf_op jit(solution)/shard_map/pallas_call | solution.py:190
  34.6 10.6 %all-to-all-start.1 = ((bf16[16,16,128]{2,1,0:T(8,128)(2,1)}), bf16[16,16,128]{2,1,0:T(8,128)(2,1)S(1)}, u32[]{:S(2)}, u32[]{:S(2)}) async-start(bf16[16,16,128]{2,1,0:T(8,128)(2,1)} %get-tuple-element.12), calls=%async_computation.1 | async-start | bytes 131072 | tf_op jit(solution)/shard_map/all_to_all | solution.py:206
  45.2 0.0 copy-done
  45.2 0.1 dynamic-slice_bitcast_fusion.skip_ref
  45.3 2.2 %shard_map.75 = (f32[8,128,128]{2,1,0:T(8,128)S(1)}, f32[16,128,128]{2,1,0:T(8,128)S(1)}) custom-call(bf16[8,256,128]{2,1,0:T(8,128)(2,1)S(1)} %all-to-all-done.slices_ref, f32[8,16,128]{2,1,0:T(8,128)S(1)} %get-tuple-element.13.states_ref, f32[16,128]{1,0:T(8,128)S(1)} %get-tuple-element.18.scale_ref, f32[16,128]{1,0:T(8,128)S(1)} %get-tuple-element.17.res_ref, ...), custom_call_target="tpu_custom_call" | custom-call | flops 20000000 | bytes 2000000 | tf_op jit(solution)/shard_map/pallas_call | solution.py:190
  47.5 9.8 %all-to-all-done.1.totals_ref = bf16[16,16,128]{2,1,0:T(8,128)(2,1)S(1)} async-done(((bf16[16,16,128]{2,1,0:T(8,128)(2,1)}), bf16[16,16,128]{2,1,0:T(8,128)(2,1)S(1)}, u32[]{:S(2)}, u32[]{:S(2)}) %all-to-all-start.1) | async-done | bytes 65568 | tf_op jit(solution)/shard_map/all_to_all | solution.py:206
  57.4 0.7 shard_map.76
  58.1 19.8 %all_to_all.20.gated_ref = bf16[8,4,128,128]{3,2,1,0:T(8,128)(2,1)S(1)} all-to-all(bf16[8,4,128,128]{3,2,1,0:T(8,128)(2,1)S(1)} %shard_map.76), channel_id=1, replica_groups=mesh['zp'=8,'zq'=2,'y'=4,'core'=2,'x'=4] {'core','y'}, dimensions={0} | all-to-all | bytes 2097152 | tf_op jit(solution)/shard_map/all_to_all | solution.py:206
  77.9 0.0 all-gather.2.cloned.1.call-done.weight_hbm
  77.9 2.7 %shard_map.77 = bf16[16,128,256]{2,1,0:T(8,128)(2,1)S(1)} custom-call(bf16[8,4,128,128]{3,2,1,0:T(8,128)(2,1)S(1)} %all_to_all.20.gated_ref, bf16[1024,1024]{1,0:T(8,128)(2,1)} %all-gather.2.cloned.1.call-done.weight_hbm), custom_call_target="tpu_custom_call" | custom-call | tf_op jit(solution)/shard_map/pallas_call | solution.py:190
  80.6 20.2 %all_to_all.21.pieces_ref = bf16[16,128,256]{2,1,0:T(8,128)(2,1)S(1)} all-to-all(bf16[16,128,256]{2,1,0:T(8,128)(2,1)S(1)} %shard_map.77), channel_id=1, replica_groups=mesh['zp'=8,'zq'=2,'y'=4,'core'=2,'x'=4] {'y','x'}, dimensions={0} | all-to-all | bytes 2097152 | tf_op jit(solution)/shard_map/all_to_all | solution.py:206
  100.9 0.9 shard_map.78
Async XLA Ops:
  6.5 38.7 %copy-start = (f32[1024]{0:T(1024)S(1)}, f32[1024]{0:T(1024)}, u32[]{:S(2)}) copy-start(f32[1024]{0:T(1024)} %param.12) | copy-start | bytes 12292
  6.5 71.3 %all-gather.2.cloned.1.call-start = ((), (), s32[]{:S(2)}) async-start(), calls=%async_computation.4 | async-start | bytes 2228224 | tf_op jit(solution)/shard_map/all_gather | solution.py:227
  6.5 6.7 %collective-permute-start = (bf16[32,1024]{1,0:T(8,128)(2,1)}, bf16[32,1024]{1,0:T(8,128)(2,1)S(1)}, u32[]{:S(2)}, u32[]{:S(2)}) collective-permute-start(bf16[32,1024]{1,0:T(8,128)(2,1)} %weight_hbm.1), channel_id=1, source_target_pairs={{0,32},{32,0},{1,33},{33,1},{2,34},{34,2},{3,35},{35,3},{4,36},{36... | collective-permute-start | bytes 196616 | tf_op jit(solution)/shard_map/ppermute | solution.py:225
  13.9 19.5 %all-to-all-start = ((bf16[8,256,128]{2,1,0:T(8,128)(2,1)}), bf16[8,256,128]{2,1,0:T(8,128)(2,1)S(1)}, u32[]{:S(2)}, u32[]{:S(2)}) async-start(bf16[8,256,128]{2,1,0:T(8,128)(2,1)} %get-tuple-element.11), calls=%async_computation | async-start | bytes 1048576 | tf_op jit(solution)/shard_map/all_to_all | solution.py:206
  34.6 22.8 %all-to-all-start.1 = ((bf16[16,16,128]{2,1,0:T(8,128)(2,1)}), bf16[16,16,128]{2,1,0:T(8,128)(2,1)S(1)}, u32[]{:S(2)}, u32[]{:S(2)}) async-start(bf16[16,16,128]{2,1,0:T(8,128)(2,1)} %get-tuple-element.12), calls=%async_computation.1 | async-start | bytes 131072 | tf_op jit(solution)/shard_map/all_to_all | solution.py:206
Sparse Core Ops, SparseCore 0:
  14.0 60.7 all-gather.1
